TPU v7x, 32 devices: a whole 2x2x4 slice. The times are simulated.
32 devices in a mesh: row: 4 (over z), col: 8 (over y, x, core).
Axes of the slice: x: 2, y: 2, z: 4, core: 2. Of those that a mesh axis runs over, the one named last changes fastest.
Arguments:
- front_panel: float32 [12288, 1024], P('row', 'col')
- front_trail: float32 [12288, 4096], P('row', 'col'), may hold values from -6 to 6
- child_panel: float32 [2, 4096, 1024], P(None, 'row', 'col'), may hold values from -0.1875 to 0.1875
- child_trail: float32 [2, 4096, 4096], P(None, 'row', 'col'), may hold values from -4 to 4
- child_map: int32 [2, 4096], P(None, 'row'), may hold values from 0 to 3071, as said below
- child_count: int32 [2, 4], P(None, 'row'), may hold values from 256 to 1024, as said below
Outputs:
- factor: float32 [12288, 1024], P('row', 'col')
- schur_block: float32 [12288, 4096], P('row', 'col')
Inputs may be any that keep to these rules, and one draw needn't show every extreme that they name: `child_map`: within each slab and each aligned block of 1024 entries the values are distinct rows of one row block. `child_count`: some slab of some row block has all 1024 rows live in every draw.
All inputs are finite; a program needn't handle non-finite values.
Results may differ from a plain program's by a relative error of at most 0.00012.
Values sent between devices are 32-bit elements; how exact they have to be, the bound alone decides.
A program may use at most 192 MiB of HBM per device.

v0:
```python
import jax
import jax.numpy as jnp
from jax import lax
from jax.sharding import PartitionSpec as P


def swapped(block, axis, distance):
    count = lax.axis_size(axis)
    route = []
    for low in range(count):
        high = low | 1 << distance
        if high != low and high < count:
            route += [(low, high), (high, low)]
    return lax.ppermute(block, axis, route)


def from_root(value, axis, root):
    mine = lax.axis_index(axis) == root
    return lax.psum(jnp.where(mine, value, jnp.zeros_like(value)), axis)


def on_device(front_panel, front_trail, child_panel, child_trail, child_map, child_count):
    block_rows, panel_cols = front_panel.shape
    trail_cols = front_trail.shape[1]
    slab_rows = child_map.shape[1]
    panel_width = panel_cols * lax.axis_size("col")
    top_bit = lax.axis_size("row").bit_length() - 2
    own_block = jnp.concatenate([front_panel, front_trail], axis=1)
    child_slabs = jnp.concatenate([child_panel, child_trail], axis=2)
    live_rows = jnp.arange(slab_rows, dtype=jnp.int32)[None, :] < child_count
    targets = jnp.where(live_rows, child_map, block_rows)
    assembled = own_block.at[targets[0]].add(child_slabs[0], mode="drop")
    partner = jnp.zeros_like(own_block).at[targets[1]].add(child_slabs[1], mode="drop")
    assembled = assembled + swapped(partner, "row", top_bit)
    assembled_panel = assembled[:, :panel_cols]
    assembled_trail = assembled[:, panel_cols:]
    row_id = lax.axis_index("row")
    col_id = lax.axis_index("col")
    first_row = row_id * block_rows
    window_start = panel_width + col_id * trail_cols
    window_root = window_start // block_rows
    window_offset = window_start - window_root * block_rows
    diag_piece = from_root(assembled_panel[:panel_width], "row", 0)
    panel_full, diag_full = (
        lax.all_gather(assembled_panel, "col", axis=1, tiled=True),
        lax.all_gather(diag_piece, "col", axis=1, tiled=True),
    )
    symmetric = 0.5 * (diag_full + diag_full.T)
    lower_factor = jnp.linalg.cholesky(symmetric)
    solved = jax.scipy.linalg.solve_triangular(lower_factor, panel_full.T, lower=True).T
    global_rows = first_row + jnp.arange(block_rows, dtype=jnp.int32)
    padded = jnp.concatenate(
        [lower_factor, jnp.zeros((block_rows - panel_width, panel_width), jnp.float32)], axis=0
    )
    factor_rows = jnp.where((global_rows < panel_width)[:, None], padded, solved)
    window_factor = from_root(
        lax.dynamic_slice_in_dim(factor_rows, window_offset, trail_cols, 0), "row", window_root
    )
    schur_block = assembled_trail - jnp.dot(
        factor_rows, window_factor.T, precision=lax.Precision.HIGHEST
    )
    factor_block = lax.dynamic_slice_in_dim(factor_rows, col_id * panel_cols, panel_cols, 1)
    return (factor_block, schur_block)


def solution(mesh):
    in_specs = (
        P("row", "col"),
        P("row", "col"),
        P(None, "row", "col"),
        P(None, "row", "col"),
        P(None, "row"),
        P(None, "row"),
    )
    out_specs = (P("row", "col"), P("row", "col"))
    return jax.shard_map(
        on_device, mesh=mesh, in_specs=in_specs, out_specs=out_specs, check_vma=False
    )
```

profile of v0, /device:TPU:20, one launch (start us, length us, event | category | flops | bytes accessed | tf_op | source)
XLA Modules:
  0.0 1092.9 jit_solution(13862431565012249729)
XLA Ops:
  10.3 4.6 constant_dynamic-update-slice_fusion
  14.9 11.7 %scatter_custom_fusion = f32[3072,640]{1,0:T(8,128)} fusion(s32[1024]{0:T(1024)S(1)} %bitcast.136, f32[]{:T(128)} %constant.295.clone.1, f32[2,1024,640]{2,1,0:T(8,128)} %constant_dynamic-update-slice_fusion), kind=kCustom, calls=%fused_computation.28 | custom fusion | flops 655360 | bytes 10486272 | tf_op jit(solution)/shard_map/scatter-add | solution.py:33
  26.9 337.3 %collective-permute-done = f32[3072,640]{1,0:T(8,128)} collective-permute-done((f32[3072,640]{1,0:T(8,128)}, f32[3072,640]{1,0:T(8,128)}, u32[]{:S(2)}, u32[]{:S(2)}) %collective-permute-start) | collective-permute-done | bytes 7864352 | tf_op jit(solution)/shard_map/ppermute | solution.py:14
  364.2 9.0 maximum_add_fusion
  373.2 14.4 %scatter_custom_fusion.1 = f32[3072,640]{1,0:T(8,128)} fusion(f32[3072,640]{1,0:T(8,128)} %maximum_add_fusion, s32[1024]{0:T(1024)S(1)} %bitcast.135, f32[2,1024,640]{2,1,0:T(8,128)} %constant_dynamic-update-slice_fusion), kind=kCustom, calls=%fused_computation.42 | custom fusion | flops 655360 | bytes 10485760 | tf_op jit(solution)/shard_map/scatter-add | solution.py:32
  389.8 42.0 %all-reduce.5.cloned.1.call-done = f32[1024,128]{0,1:T(8,128)} async-done(((f32[1024,128]{0,1:T(8,128)}), f32[1024,128]{0,1:T(8,128)}) %all-reduce.5.cloned.1.call-update) | async-done | bytes 524304 | tf_op jit(solution)/shard_map/psum | solution.py:19
  434.7 35.9 %all-gather.3.cloned.1.call-done = f32[1024,1024]{0,1:T(8,128)} async-done(((f32[1024,128]{0,1:T(8,128)}), f32[1024,1024]{0,1:T(8,128)}) %all-gather.3.cloned.1.call-update) | async-done | bytes 4194320 | tf_op jit(solution)/shard_map/all_gather | solution.py:46
  470.6 5.3 copy.25
  475.9 6.9 fusion.15
  482.8 5.7 copy.26
  488.6 4.4 fusion.14
  495.0 11.7 %cholesky.223 = f32[128,128]{1,0:T(8,128)S(1)} custom-call(f32[128,128]{1,0:T(8,128)S(1)} %cholesky.580), custom_call_target="Cholesky" | custom-call | tf_op jit(solution)/shard_map/jit(cholesky)/cholesky | solution.py:49
  509.7 9.8 custom-call.63
  523.4 12.1 %cholesky.244 = f32[128,128]{1,0:T(8,128)S(1)} custom-call(f32[128,128]{1,0:T(8,128)S(1)} %cholesky.584), custom_call_target="Cholesky" | custom-call | tf_op jit(solution)/shard_map/jit(cholesky)/cholesky | solution.py:49
  536.1 9.8 custom-call.64
  549.2 11.7 %cholesky.468 = f32[128,128]{1,0:T(8,128)S(1)} custom-call(f32[128,128]{1,0:T(8,128)S(1)} %cholesky.589), custom_call_target="Cholesky" | custom-call | tf_op jit(solution)/shard_map/jit(cholesky)/cholesky | solution.py:49
  561.6 9.8 custom-call.65
  574.9 11.9 %cholesky.487 = f32[128,128]{1,0:T(8,128)S(1)} custom-call(f32[128,128]{1,0:T(8,128)S(1)} %cholesky.594), custom_call_target="Cholesky" | custom-call | tf_op jit(solution)/shard_map/jit(cholesky)/cholesky | solution.py:49
  587.4 9.8 custom-call.66
  600.6 11.7 %cholesky.506 = f32[128,128]{1,0:T(8,128)S(1)} custom-call(f32[128,128]{1,0:T(8,128)S(1)} %cholesky.599), custom_call_target="Cholesky" | custom-call | tf_op jit(solution)/shard_map/jit(cholesky)/cholesky | solution.py:49
  613.0 10.0 custom-call.67
  626.3 11.7 %cholesky.526 = f32[128,128]{1,0:T(8,128)S(1)} custom-call(f32[128,128]{1,0:T(8,128)S(1)} %cholesky.604), custom_call_target="Cholesky" | custom-call | tf_op jit(solution)/shard_map/jit(cholesky)/cholesky | solution.py:49
  638.6 9.8 custom-call.68
  651.5 11.7 %cholesky.546 = f32[128,128]{1,0:T(8,128)S(1)} custom-call(f32[128,128]{1,0:T(8,128)S(1)} %cholesky.609), custom_call_target="Cholesky" | custom-call | tf_op jit(solution)/shard_map/jit(cholesky)/cholesky | solution.py:49
  663.8 9.8 custom-call.69
  676.3 11.7 %cholesky.564 = f32[128,128]{1,0:T(8,128)S(1)} custom-call(f32[128,128]{1,0:T(8,128)S(1)} %convolution_subtract_fusion.11), custom_call_target="Cholesky" | custom-call | tf_op jit(solution)/shard_map/jit(cholesky)/cholesky | solution.py:49
  698.2 6.8 fusion.16
  705.0 23.6 %while.1 = (s32[]{:T(128)}, f32[1024,1024]{1,0:T(8,128)}, s32[8,2]{0,1:T(2,128)S(1)}, f32[8,128,128]{2,1,0:T(8,128)S(1)}, s32[]{:T(128)}) while((s32[]{:T(128)}, f32[1024,1024]{1,0:T(8,128)}, s32[8,2]{0,1:T(2,128)S(1)}, f32[8,128,128]{2,1,0:T(8,128)S(1)}, s32[]{:T(128)}) %tuple.60), condition=%wide.while_cond, body=%wide.while_body.sunk | while | flops 2 | bytes 131181 | solution.py:50
  728.6 78.8 %custom-call.70 = f32[8,128,128]{1,2,0:T(8,128)S(1)} custom-call(f32[8,128,128]{2,1,0:T(8,128)S(1)} %get-tuple-element.9), custom_call_target="InvertDiagBlocksLowerTriangular" | custom-call | tf_op jit(solution)/shard_map/jit(_solve_triangular)/triangular_solve | solution.py:50
  807.4 5.4 constant_dynamic-update-slice_fusion.19
  812.9 4.1 convolution_subtract_fusion.1
  817.0 4.8 constant_dynamic-update-slice_fusion.18
  821.8 6.7 convolution_subtract_fusion.4
  828.5 5.0 constant_dynamic-update-slice_fusion.17
  833.5 10.2 fusion.19
  843.7 4.7 constant_dynamic-update-slice_fusion.16
  849.6 13.3 %fusion.22 = f32[128,3072]{0,1:T(8,128)} fusion(f32[128,3072]{1,0:T(8,128)S(1)} %get-tuple-element.70, f32[128,3072]{1,0:T(8,128)S(1)} %get-tuple-element.69, f32[128,3072]{1,0:T(8,128)S(1)} %get-tuple-element.68, f32[128,3072]{1,0:T(8,128)S(1)} %get-tuple-element.67, f32[1024,3072]{0,1:T(8,128)} %bitcast.131, f32[1024,1024]{1,0:T(8,128)} %get-tuple-element.127), kind=kOutput, calls=%fused_computation.37 | convolution fusion | flops 2421030912 | bytes 9699328 | tf_op jit(solution)/shard_map/jit(_solve_triangular)/triangular_solve | solution.py:50
  872.2 5.2 constant_dynamic-update-slice_fusion.15
  877.4 15.7 %convolution_subtract_fusion.3 = f32[128,3072]{0,1:T(8,128)S(1)} fusion(f32[640,3072]{1,0:T(8,128)} %get-tuple-element.28, f32[1024,3072]{0,1:T(8,128)} %bitcast.132, f32[1024,1024]{1,0:T(8,128)} %get-tuple-element.127), kind=kOutput, calls=%fused_computation.34 | convolution fusion | flops 3020292096 | bytes 11337728 | tf_op jit(solution)/shard_map/jit(_solve_triangular)/triangular_solve | solution.py:50
  893.1 4.1 constant_dynamic-update-slice_fusion.14
  897.2 17.9 %convolution_subtract_fusion = f32[128,3072]{0,1:T(8,128)S(1)} fusion(f32[768,3072]{1,0:T(8,128)} %get-tuple-element.25, f32[1024,3072]{0,1:T(8,128)} %bitcast.133, f32[1024,1024]{1,0:T(8,128)} %get-tuple-element.127), kind=kOutput, calls=%fused_computation.31 | convolution fusion | flops 3624271872 | bytes 12976128 | tf_op jit(solution)/shard_map/jit(_solve_triangular)/triangular_solve | solution.py:50
  915.1 3.6 constant_dynamic-update-slice_fusion.13
  918.7 21.2 %convolution_subtract_fusion.2 = f32[128,3072]{0,1:T(8,128)} fusion(f32[896,3072]{1,0:T(8,128)} %get-tuple-element.73, f32[1024,3072]{0,1:T(8,128)} %bitcast.134, f32[1024,1024]{1,0:T(8,128)} %get-tuple-element.127), kind=kOutput, calls=%fused_computation.33 | convolution fusion | flops 4228251648 | bytes 14614528 | tf_op jit(solution)/shard_map/jit(_solve_triangular)/triangular_solve | solution.py:50
  957.2 3.4 convolution_dynamic-update-slice_fusion
  960.6 11.4 %bitcast_select_fusion = f32[3072,1024]{1,0:T(8,128)} fusion(f32[1024,3072]{0,1:T(8,128)} %convolution_dynamic-update-slice_fusion, f32[1024,1024]{1,0:T(8,128)} %get-tuple-element.21, pred[3072]{0:T(1024)(128)(4,1)S(1)} %add_compare_fusion), kind=kLoop, calls=%fused_computation.4 | loop fusion | flops 3145728 | bytes 29363200 | tf_op jit(solution)/shard_map/jit(_where)/select_n | solution.py:55
  972.0 3.2 dynamic-slice_select_fusion
  977.9 83.1 %all-reduce.7.cloned.1.call-done = f32[512,1024]{1,0:T(8,128)} async-done(((f32[512,1024]{1,0:T(8,128)}), f32[512,1024]{1,0:T(8,128)}) %all-reduce.7.cloned.1.call-update) | async-done | bytes 2097168 | tf_op jit(solution)/shard_map/psum | solution.py:19
  1061.0 24.9 %slice_subtract_fusion = f32[3072,512]{1,0:T(8,128)} fusion(f32[3072,640]{1,0:T(8,128)} %scatter_custom_fusion.1, f32[3072,1024]{1,0:T(8,128)} %bitcast_select_fusion, f32[512,1024]{1,0:T(8,128)} %all-reduce.7.cloned.1.call-done), kind=kOutput, calls=%fused_computation.6 | convolution fusion | flops 19328925696 | bytes 27262976 | tf_op jit(solution)/shard_map/dot_general | solution.py:59
  (123 shorter events, 99.4 us)
Async XLA Ops:
  7.2 424.6 %all-reduce.5.cloned.1.call-start = ((), (), s32[]{:S(2)}) async-start(), calls=%async_computation | async-start | bytes 1048576 | tf_op jit(solution)/shard_map/psum | solution.py:19
  14.9 349.3 %copy-start.10 = (f32[3072,128]{1,0:T(8,128)S(1)}, f32[3072,128]{1,0:T(8,128)}, u32[]{:S(2)}) copy-start(f32[3072,128]{1,0:T(8,128)} %param.6) | copy-start | bytes 4718596
  26.6 337.7 %collective-permute-start = (f32[3072,640]{1,0:T(8,128)}, f32[3072,640]{1,0:T(8,128)}, u32[]{:S(2)}, u32[]{:S(2)}) collective-permute-start(f32[3072,640]{1,0:T(8,128)} %scatter_custom_fusion), channel_id=1, source_target_pairs={{0,16},{16,0},{8,24},{24,8},{1,17},{17,1},{9,25},{25,9},{2,18},{18... | collective-permute-start | bytes 23592968 | tf_op jit(solution)/shard_map/ppermute | solution.py:14
  389.7 80.9 %all-gather.3.cloned.1.call-start = ((), (), s32[]{:S(2)}) async-start(), calls=%async_computation.1 | async-start | bytes 4718592 | tf_op jit(solution)/shard_map/all_gather | solution.py:46
  431.8 375.6 %all-gather.5.cloned.1.call-start = ((), (), s32[]{:S(2)}) async-start(), calls=%async_computation.2 | async-start | bytes 14155776 | tf_op jit(solution)/shard_map/all_gather | solution.py:45
  434.5 626.4 %all-reduce.7.cloned.1.call-start = ((), (), s32[]{:S(2)}) async-start(), calls=%async_computation.3 | async-start | bytes 4194304 | tf_op jit(solution)/shard_map/psum | solution.py:19
  493.0 2.0 copy-start.1
  807.4 9.6 copy-start.12
  833.5 14.9 %copy-start = (f32[128,3072]{1,0:T(8,128)}, f32[128,3072]{1,0:T(8,128)S(1)}, u32[]{:S(2)}) copy-start(f32[128,3072]{1,0:T(8,128)S(1)} %get-tuple-element.69) | copy-start | bytes 4718596
  848.5 1.1 copy-start.9
  870.6 1.6 copy-start.11
  941.5 7.6 copy-start.4
  943.1 7.4 copy-start.3
  946.2 5.6 copy-start.2
  949.1 4.0 copy-start.8
  950.5 4.0 copy-start.7
  951.8 4.1 copy-start.6
  953.2 4.0 copy-start.5
Sparse Core Ops, SparseCore 0:
  389.9 41.8 all-reduce.4
  433.7 36.8 all-gather.2
  473.1 73.9 all-gather.4
  975.3 85.6 all-reduce.6
where the time goes:
time: 1100 us; the launch traced here: 1090 us
  waiting for transfers between devices  498 us (45%)
  other arithmetic  320 us (29%)
  matrix products  173 us (16%)
  local copies, waits for them, and re-layouts  80.7 us (7%)
  between operations  19.6 us (2%)
    ppermute x1, waiting for transfers between devices, swapped(): return lax.ppermute(block, axis, route)  337 us
    another operation x30, other arithmetic, on_device(): lower_factor = jnp.linalg.cholesky(symmetric)  172 us
    another operation x15, matrix products, on_device(): jax.scipy.linalg.solve_triangular(lower_factor, panel_full.T, lower=True)  125 us
    psum x2, waiting for transfers between devices, from_root(): return lax.psum(jnp.where(mine, value, jnp.zeros_like(value)), axis)  125 us
    another operation x3, other arithmetic, on_device(): jax.scipy.linalg.solve_triangular(lower_factor, panel_full.T, lower=True)  85.6 us
    all_gather x1, waiting for transfers between devices, on_device(): lax.all_gather(diag_piece, 'col', axis=1, tiled=True)  35.9 us
    dot_general x1, matrix products, on_device(): jnp.dot(factor_rows, window_factor.T, precision=lax.Precision.HIGHEST)  24.9 us
    another operation x24, local copies, waits for them, and re-layouts  23.4 us
  transfers between devices with their start and end apart: 5, of which 4 were waited for; matrix products, arithmetic and copies ran while one was open for 31% of the time, Pallas kernels for 0%

commit v1 on v0

v1 whole, which is shorter than its diff:
```python
import functools

import jax
import jax.numpy as jnp
from jax import lax
from jax.experimental import pallas as pl
from jax.experimental.pallas import tpu as pltpu
from jax.sharding import PartitionSpec as P

HIGHEST = lax.Precision.HIGHEST
TILE = 128
GROUP = 8


def dot_tn(a, b, precision=HIGHEST):
    return lax.dot_general(
        a, b, (((0,), (0,)), ((), ())), precision=precision, preferred_element_type=jnp.float32
    )


def dot_nt(a, b, precision=HIGHEST):
    return lax.dot_general(
        a, b, (((1,), (1,)), ((), ())), precision=precision, preferred_element_type=jnp.float32
    )


def dot_nn(a, b, precision=HIGHEST):
    return jnp.dot(a, b, precision=precision, preferred_element_type=jnp.float32)


def factor_tile(tile):
    row = lax.broadcasted_iota(jnp.int32, (GROUP, TILE), 0)
    lane = lax.broadcasted_iota(jnp.int32, (GROUP, TILE), 1)
    groups = TILE // GROUP
    left = [tile[GROUP * g : GROUP * (g + 1), :] for g in range(groups)]
    right = [jnp.where(lane == row + GROUP * g, 1.0, 0.0) for g in range(groups)]
    for g in range(groups):
        a, x = left[g], right[g]
        cols = [
            jnp.broadcast_to(a[:, GROUP * g + i : GROUP * g + i + 1], (GROUP, TILE))
            for i in range(GROUP)
        ]
        for i in range(GROUP):
            pivot = jnp.broadcast_to(cols[i][i : i + 1, :], (GROUP, TILE))
            scale = lax.rsqrt(pivot)
            column = cols[i] * scale
            below = jnp.where(row > i, column, 0.0)
            a_row = jnp.broadcast_to(a[i : i + 1, :], (GROUP, TILE)) * scale
            x_row = jnp.broadcast_to(x[i : i + 1, :], (GROUP, TILE)) * scale
            a = jnp.where(row == i, a_row, a - below * a_row)
            x = jnp.where(row == i, x_row, x - below * x_row)
            for k in range(i + 1, GROUP):
                cols[k] = cols[k] - below * jnp.broadcast_to(column[k : k + 1, :], (GROUP, TILE))
        a = jnp.where(lane >= row + GROUP * g, a, 0.0)
        left[g], right[g] = a, x
        if g + 1 < groups:
            change = dot_tn(a, jnp.concatenate([a, x], axis=1))
            for h in range(g + 1, groups):
                part = change[GROUP * h : GROUP * (h + 1), :]
                left[h] = left[h] - part[:, :TILE]
                right[h] = right[h] - part[:, TILE:]
    return jnp.concatenate(left, axis=0), jnp.concatenate(right, axis=0)


def cholesky_kernel(diag_ref, upper_ref, inverse_ref):
    size = diag_ref.shape[0]
    count = size // TILE
    for i in range(count):
        for j in range(i, count):
            here = diag_ref[TILE * i : TILE * (i + 1), TILE * j : TILE * (j + 1)]
            there = diag_ref[TILE * j : TILE * (j + 1), TILE * i : TILE * (i + 1)]
            inverse_ref[TILE * i : TILE * (i + 1), TILE * j : TILE * (j + 1)] = 0.5 * (
                here + there.T
            )
        if i:
            inverse_ref[TILE * i : TILE * (i + 1), : TILE * i] = jnp.zeros(
                (TILE, TILE * i), jnp.float32
            )
    block = lax.broadcasted_iota(jnp.int32, (TILE, size), 1) // TILE

    def step(b, carry):
        at = pl.multiple_of(b * TILE, TILE)
        rows, cols = pl.ds(at, TILE), pl.ds(at, TILE)
        top, inv = factor_tile(inverse_ref[rows, cols])
        scaled = dot_nn(inv, inverse_ref[rows, :])
        upper_ref[rows, :] = jnp.where(block > b, scaled, 0.0)
        upper_ref[rows, cols] = top
        inverse_ref[rows, :] = scaled
        inverse_ref[rows, cols] = inv

        def below(s, inner):
            under = pl.ds(pl.multiple_of(s * TILE, TILE), TILE)
            change = dot_tn(upper_ref[rows, under], inverse_ref[rows, :])
            inverse_ref[under, :] = jnp.where(block == b, 0.0, inverse_ref[under, :]) - change
            return inner

        lax.fori_loop(b + 1, count, below, 0)
        inverse_ref[rows, :] = jnp.where(block <= b, inverse_ref[rows, :], 0.0)
        return carry

    lax.fori_loop(0, count, step, 0)


def cholesky(diag):
    size = diag.shape[0]
    shape = jax.ShapeDtypeStruct((size, size), jnp.float32)
    return pl.pallas_call(
        cholesky_kernel,
        out_shape=(shape, shape),
        in_specs=[pl.BlockSpec(memory_space=pltpu.VMEM)],
        out_specs=(pl.BlockSpec(memory_space=pltpu.VMEM),) * 2,
        compiler_params=pltpu.CompilerParams(vmem_limit_bytes=40 << 20),
        cost_estimate=pl.CostEstimate(
            flops=60_000_000_000, bytes_accessed=12 * size * size, transcendentals=0
        ),
        name="cholesky_and_inverse",
    )(diag)


def halves(value):
    high = value.astype(jnp.bfloat16)
    return high, (value - high.astype(jnp.float32)).astype(jnp.bfloat16)


def update_kernel(
    top_tiles, root_ref, panel_ref, right_ref, trail_ref, window_ref, lower_ref,
    factor_ref, schur_ref, high_ref, low_ref,
):
    step = pl.program_id(0)
    width = trail_ref.shape[1]

    @pl.when(step == 0)
    def _():
        high, low = halves(right_ref[...])
        high_ref[...] = high
        low_ref[...] = low

    in_top = jnp.logical_and(root_ref[0] == 1, step < top_tiles)

    @pl.when(in_top)
    def _():
        factor_ref[...] = lower_ref[...]
        schur_ref[...] = trail_ref[...] - window_ref[...]

    @pl.when(jnp.logical_not(in_top))
    def _():
        high, low = halves(panel_ref[...])
        product = (
            dot_nn(high, low_ref[...], None) + dot_nn(low, high_ref[...], None)
        ) + dot_nn(high, high_ref[...], None)
        factor_ref[...] = product[:, width:]
        schur_ref[...] = trail_ref[...] - product[:, :width]


def update(root, panel, right, trail, window, lower):
    rows, depth = panel.shape
    width, narrow = trail.shape[1], lower.shape[1]
    size = 512
    top_tiles = depth // size

    def capped(i, root):
        return jnp.minimum(i, top_tiles - 1), 0

    return pl.pallas_call(
        functools.partial(update_kernel, top_tiles),
        grid_spec=pltpu.PrefetchScalarGridSpec(
            num_scalar_prefetch=1,
            grid=(rows // size,),
            in_specs=[
                pl.BlockSpec((size, depth), lambda i, root: (i, 0)),
                pl.BlockSpec((depth, width + narrow), lambda i, root: (0, 0)),
                pl.BlockSpec((size, width), lambda i, root: (i, 0)),
                pl.BlockSpec((size, width), capped),
                pl.BlockSpec((size, narrow), capped),
            ],
            out_specs=(
                pl.BlockSpec((size, narrow), lambda i, root: (i, 0)),
                pl.BlockSpec((size, width), lambda i, root: (i, 0)),
            ),
            scratch_shapes=[pltpu.VMEM((depth, width + narrow), jnp.bfloat16)] * 2,
        ),
        out_shape=(
            jax.ShapeDtypeStruct((rows, narrow), jnp.float32),
            jax.ShapeDtypeStruct((rows, width), jnp.float32),
        ),
        compiler_params=pltpu.CompilerParams(vmem_limit_bytes=48 << 20),
        name="factor_and_schur",
    )(root, panel, right, trail, window, lower)


def swapped(block, axis, distance):
    count = lax.axis_size(axis)
    route = []
    for low in range(count):
        high = low | 1 << distance
        if high != low and high < count:
            route += [(low, high), (high, low)]
    return lax.ppermute(block, axis, route)


def on_device(front_panel, front_trail, child_panel, child_trail, child_map, child_count):
    block_rows, panel_cols = front_panel.shape
    trail_cols = front_trail.shape[1]
    slab_rows = child_map.shape[1]
    panel_width = panel_cols * lax.axis_size("col")
    top_bit = lax.axis_size("row").bit_length() - 2
    row_id = lax.axis_index("row")
    col_id = lax.axis_index("col")
    live_rows = jnp.arange(slab_rows, dtype=jnp.int32)[None, :] < child_count
    targets = jnp.where(live_rows, child_map, block_rows)

    own_panel = front_panel.at[targets[0]].add(child_panel[0], mode="drop")
    partner_top = jnp.zeros((panel_width, panel_cols), jnp.float32).at[targets[1]].add(
        child_panel[1], mode="drop"
    )
    share = jnp.where(
        row_id == 0,
        own_panel[:panel_width],
        jnp.where(row_id == 1 << top_bit, partner_top, 0.0),
    )
    diag_piece = lax.psum(share, "row")
    diag_full = lax.all_gather(diag_piece, "col", axis=1, tiled=True)

    partner_targets = swapped(targets[1], "row", top_bit)
    panel_slab = swapped(child_panel[1], "row", top_bit)
    trail_slab = swapped(child_trail[1], "row", top_bit)
    panel = own_panel.at[partner_targets].add(panel_slab, mode="drop")
    panel_full = lax.all_gather(panel, "col", axis=1, tiled=True)
    trail = front_trail.at[targets[0]].add(child_trail[0], mode="drop")
    trail = trail.at[partner_targets].add(trail_slab, mode="drop")

    window_start = panel_width + col_id * trail_cols
    window_root = window_start // block_rows
    window_rows = lax.dynamic_slice_in_dim(
        panel_full, window_start - window_root * block_rows, trail_cols, 0
    )
    window_rows, _ = lax.optimization_barrier((window_rows, diag_piece))
    window = lax.psum(jnp.where(row_id == window_root, window_rows, 0.0), "row")

    upper, inverse = cholesky(diag_full)
    first = dot_nt(inverse, window)
    second = dot_tn(inverse, first)
    own_inverse = lax.dynamic_slice_in_dim(inverse, col_id * panel_cols, panel_cols, 0)
    own_upper = lax.dynamic_slice_in_dim(upper, col_id * panel_cols, panel_cols, 0)
    right = jnp.concatenate([second, own_inverse.T], axis=1)
    root = (row_id == 0).astype(jnp.int32)[None]
    return update(root, panel_full, right, trail, window.T, own_upper.T)


def solution(mesh):
    in_specs = (
        P("row", "col"),
        P("row", "col"),
        P(None, "row", "col"),
        P(None, "row", "col"),
        P(None, "row"),
        P(None, "row"),
    )
    out_specs = (P("row", "col"), P("row", "col"))
    return jax.shard_map(
        on_device, mesh=mesh, in_specs=in_specs, out_specs=out_specs, check_vma=False
    )
```

time: 1100 us -> 350 us (0.32)
  waiting for transfers between devices: 498 us -> 107 us
  other arithmetic: 320 us -> 47.3 us
  matrix products: 173 us -> 16.4 us
  Pallas kernels: 0 us -> 110 us
  local copies, waits for them, and re-layouts: 80.7 us -> 45.8 us
    another operation x34 -> x0, other arithmetic: 267 us -> none  [the longest x30 172 us: on_device(): lower_factor = jnp.linalg.cholesky(symmetric)]
    ppermute x1 -> x3, waiting for transfers between devices: 337 us -> 88.2 us  [swapped(): return lax.ppermute(block, axis, route)]
    another operation x29 -> x0, matrix products: 148 us -> none  [the longest x15 125 us: on_device(): jax.scipy.linalg.solve_triangular(lower_factor, panel_full.T, lower=True)]
    pallas_call x0 -> x2, Pallas kernels: none -> 110 us  [the longest x1 90.9 us: cholesky(): pl.pallas_call(cholesky_kernel, out_shape=(shape, shape), in_specs=[pl.Bl...]
    psum x2, waiting for transfers between devices: 125 us -> 18.7 us  [the longest x1 18.7 us: on_device(): diag_piece = lax.psum(share, 'row')]
    another operation x40 -> x0, local copies, waits for them, and re-layouts: 42.1 us -> none
    all_gather x2, waiting for transfers between devices: 36 us -> 0.03 us  [the longest x1 0.03 us: on_device(): diag_full = lax.all_gather(diag_piece, 'col', axis=1, tiled=True)]
    scatter-add x2 -> x5, other arithmetic: 26.1 us -> 44.7 us  [the longest x1 12.8 us: on_device(): trail = front_trail.at[targets[0]].add(child_trail[0], mode='drop')]
  transfers between devices with their start and end apart: 5 -> 7, of which waited for: 4 -> 3; matrix products, arithmetic and copies ran while one was open for 31% -> 23% of each run, Pallas kernels for 0% -> 26%
where the time goes in v1:
time: 350 us; the launch traced here: 347 us
  Pallas kernels  110 us (31%)
  waiting for transfers between devices  107 us (31%)
  other arithmetic  47.3 us (14%)
  local copies, waits for them, and re-layouts  45.8 us (13%)
  matrix products  16.4 us (5%)
  between operations  15.7 us (4%)
  starting transfers between devices  4.01 us (1%)
    pallas_call x1, Pallas kernels, cholesky(): pl.pallas_call(cholesky_kernel, out_shape=(shape, shape), in_specs=[pl.Bl...  90.9 us
    ppermute x3, waiting for transfers between devices, swapped(): return lax.ppermute(block, axis, route)  88.2 us
    pallas_call x1, Pallas kernels, update(): pl.pallas_call(functools.partial(update_kernel, top_tiles), grid_spec=plt...  19.3 us
    psum x1, waiting for transfers between devices, on_device(): diag_piece = lax.psum(share, 'row')  18.7 us
    unnamed x19, local copies, waits for them, and re-layouts  13.9 us
    scatter-add x1, other arithmetic, on_device(): trail = front_trail.at[targets[0]].add(child_trail[0], mode='drop')  12.8 us
    all_gather x1, local copies, waits for them, and re-layouts, on_device(): panel_full = lax.all_gather(panel, 'col', axis=1, tiled=True)  12.6 us
    scatter-add x1, other arithmetic, on_device(): trail = trail.at[partner_targets].add(trail_slab, mode='drop')  12 us
  transfers between devices with their start and end apart: 7, of which 3 were waited for; matrix products, arithmetic and copies ran while one was open for 23% of the time, Pallas kernels for 26%

profile of v1, /device:TPU:20, one launch (start us, length us, event | category | flops | bytes accessed | tf_op | source)
XLA Modules:
  0.0 346.5 jit_solution(1484726850166480454)
XLA Ops:
  8.0 0.0 all-reduce.3.cloned.1.call-start
  8.0 0.0 copy-start.6
  8.1 6.3 %copy.29 = f32[3072,512]{1,0:T(8,128)} copy(f32[3072,512]{1,0:T(8,128)} %param.7) | data formatting | bytes 12582912
  14.4 0.0 copy-done.6
  14.4 0.8 slice_bitcast_fusion.1
  15.3 0.3 collective-permute-start.1
  15.6 0.0 copy-done.7
  15.6 0.1 compare_select_fusion.2
  15.7 6.7 %scatter_custom_fusion = f32[3072,128]{1,0:T(8,128)S(1)} fusion(f32[3072,128]{1,0:T(8,128)S(1)} %copy-done.5, s32[1024]{0:T(1024)S(1)} %bitcast.33, f32[2,1024,128]{2,1,0:T(8,128)S(1)} %copy-done.6), kind=kCustom, calls=%fused_computation.12 | custom fusion | flops 131072 | bytes 2097152 | tf_op jit(solution)/shard_map/scatter-add | solution.py:212
  22.4 6.2 %scatter_custom_fusion.2 = f32[1024,128]{1,0:T(8,128)S(1)} fusion(s32[1024]{0:T(1024)S(1)} %bitcast.35, f32[]{:T(128)} %constant.15.clone.1, f32[2,1024,128]{2,1,0:T(8,128)S(1)} %copy-done.6), kind=kCustom, calls=%fused_computation.18 | custom fusion | flops 131072 | bytes 1048580 | tf_op jit(solution)/shard_map/scatter-add | solution.py:213
  28.6 0.9 slice_select_fusion
  29.4 0.0 all-reduce.3.cloned.1.call-update
  29.4 0.0 all-gather.3.cloned.1.call-start
  29.5 2.7 collective-permute-start
  32.2 11.6 %collective-permute-done = s32[1024]{0:T(1024)S(1)} collective-permute-done((s32[1024]{0:T(1024)S(1)}, s32[1024]{0:T(1024)S(1)}, u32[]{:S(2)}, u32[]{:S(2)}) %collective-permute-start) | collective-permute-done | bytes 4128 | tf_op jit(solution)/shard_map/ppermute | solution.py:198
  43.8 0.0 collective-permute-done.1
  43.8 7.0 %scatter_fusion = f32[3072,128]{1,0:T(8,128)S(1)} fusion(f32[3072,128]{1,0:T(8,128)S(1)} %scatter_custom_fusion, s32[1024]{0:T(1024)S(1)} %compare_select_fusion.3, f32[1024,128]{1,0:T(8,128)} %collective-permute-done.1), kind=kCustom, calls=%fused_computation.1 | custom fusion | flops 131072 | bytes 1576960 | tf_op jit(solution)/shard_map/scatter-add | solution.py:227
  50.8 1.6 copy.14
  52.4 0.0 all-gather.3.cloned.1.call-update
  52.4 0.0 all-gather.5.cloned.1.call-start
  52.5 18.7 %all-reduce.3.cloned.1.call-done = f32[1024,128]{1,0:T(8,128)} async-done(((f32[1024,128]{1,0:T(8,128)}), f32[1024,128]{1,0:T(8,128)}) %all-reduce.3.cloned.1.call-update) | async-done | bytes 524304 | tf_op jit(solution)/shard_map/psum | solution.py:221
  71.2 0.0 all-gather.5.cloned.1.call-update
  71.2 0.0 all-reduce.5.cloned.1.call-start
  71.3 3.1 slice_bitcast_fusion
  74.4 0.9 collective-permute-start.2
  75.2 12.8 %scatter_custom_fusion.3 = f32[3072,512]{1,0:T(8,128)} fusion(f32[3072,512]{1,0:T(8,128)} %copy.29, s32[1024]{0:T(1024)S(1)} %bitcast.34, f32[2,1024,512]{2,1,0:T(8,128)} %param.9), kind=kCustom, calls=%fused_computation.6 | custom fusion | flops 524288 | bytes 8388608 | tf_op jit(solution)/shard_map/scatter-add | solution.py:229
  88.0 76.6 %collective-permute-done.2 = f32[1024,512]{1,0:T(8,128)S(1)} collective-permute-done((f32[1024,512]{1,0:T(8,128)}, f32[1024,512]{1,0:T(8,128)S(1)}, u32[]{:S(2)}, u32[]{:S(2)}) %collective-permute-start.2) | collective-permute-done | bytes 2097184 | tf_op jit(solution)/shard_map/ppermute | solution.py:198
  164.7 12.0 %scatter_fusion.1 = f32[3072,512]{1,0:T(8,128)} fusion(f32[3072,512]{1,0:T(8,128)} %scatter_custom_fusion.3, s32[1024]{0:T(1024)S(1)} %compare_select_fusion.3, f32[1024,512]{1,0:T(8,128)S(1)} %collective-permute-done.2), kind=kCustom, calls=%fused_computation.4 | custom fusion | flops 524288 | bytes 6295552 | tf_op jit(solution)/shard_map/scatter-add | solution.py:230
  176.7 1.8 constant_dynamic-slice_fusion
  178.4 1.5 broadcast_select_fusion
  180.0 0.0 all-reduce.5.cloned.1.call-update
  180.0 0.0 all-gather.5.cloned.1.call-done.diag_ref
  180.0 0.0 copy-start.4
  180.0 2.2 copy-done.4
  182.2 90.9 %cholesky_and_inverse.1 = (f32[1024,1024]{1,0:T(8,128)S(1)}, f32[1024,1024]{1,0:T(8,128)S(1)}) custom-call(f32[1024,1024]{1,0:T(8,128)S(1)} %copy-done.4), custom_call_target="tpu_custom_call" | custom-call | flops 60000002048 | bytes 12582912 | tf_op jit(solution)/shard_map/cholesky_and_inverse/pallas_call | solution.py:107
  273.2 2.0 copy-done
  275.2 2.0 copy-done.3
  277.2 5.4 %copy.15 = f32[1024,1024]{0,1:T(8,128)} copy(f32[1024,1024]{1,0:T(8,128)} %copy-done) | data formatting | bytes 8388608 | tf_op jit(solution)/shard_map/cholesky_and_inverse/pallas_call | solution.py:107
  282.5 5.3 %copy.17 = f32[1024,1024]{0,1:T(8,128)} copy(f32[1024,1024]{1,0:T(8,128)} %copy-done.3) | data formatting | bytes 8388608 | tf_op jit(solution)/shard_map/cholesky_and_inverse/pallas_call | solution.py:107
  287.9 1.3 dynamic-slice_bitcast_fusion
  289.2 12.6 %copy.18.panel_ref = f32[3072,1024]{1,0:T(8,128)} copy(f32[3072,1024]{0,1:T(8,128)} %all-gather.3.cloned.1.call-done) | data formatting | bytes 25165824 | tf_op jit(solution)/shard_map/all_gather | solution.py:228
  301.8 9.6 %fusion.8 = f32[1024,512]{1,0:T(8,128)S(1)} fusion(f32[1024,1024]{1,0:T(8,128)} %copy-done, f32[512,1024]{0,1:T(8,128)} %all-reduce.5.cloned.1.call-done), kind=kOutput, calls=%fused_computation.26 | convolution fusion | flops 6442450944 | bytes 8388608 | tf_op jit(solution)/shard_map/dot_general | solution.py:22
  311.4 0.0 copy-done.1
  311.4 6.8 %fusion.9 = f32[1024,512]{1,0:T(8,128)S(1)} fusion(f32[1024,1024]{1,0:T(8,128)S(1)} %copy-done.1, f32[1024,512]{1,0:T(8,128)S(1)} %fusion.8), kind=kOutput, calls=%fused_computation.27 | convolution fusion | flops 6442450944 | bytes 8388608 | tf_op jit(solution)/shard_map/dot_general | solution.py:16
  318.2 0.0 copy-start.2
  318.2 0.2 pad_maximum_fusion.right_ref
  318.4 1.4 copy-done.2
  319.8 19.3 %factor_and_schur.1 = (f32[3072,128]{1,0:T(8,128)}, f32[3072,512]{1,0:T(8,128)}) custom-call(s32[1]{0:T(128)} %bitcast.root_ref, f32[3072,1024]{1,0:T(8,128)} %copy.18.panel_ref, f32[1024,640]{1,0:T(8,128)S(1)} %pad_maximum_fusion.right_ref, f32[3072,512]{1,0:T(8,128)} %scatter_fusion.1, f32[1024,512]{1,0:T(8,128)S(1)} %bitcast.31, ...), custom_call_target="tpu_custom_call" | custom-call | tf_op jit(solution)/shard_map/factor_and_schur/pallas_call | solution.py:164
  (13 shorter events, 0.0 us)
Async XLA Ops:
  8.0 63.2 %all-reduce.3.cloned.1.call-start = ((), (), s32[]{:S(2)}) async-start(), calls=%async_computation.1 | async-start | bytes 1048576 | tf_op jit(solution)/shard_map/psum | solution.py:221
  8.0 6.4 %copy-start.6 = (f32[2,1024,128]{2,1,0:T(8,128)S(1)}, f32[2,1024,128]{2,1,0:T(8,128)}, u32[]{:S(2)}) copy-start(f32[2,1024,128]{2,1,0:T(8,128)} %param.8) | copy-start | bytes 3145732
  8.1 7.5 %copy-start.7 = (s32[2,1024]{1,0:T(2,128)S(1)}, s32[2,1024]{1,0:T(2,128)}, u32[]{:S(2)}) copy-start(s32[2,1024]{1,0:T(2,128)} %param.10) | copy-start | bytes 24580
  8.1 7.5 %copy-start.8 = (s32[2,1]{0,1:T(1,128)S(1)}, s32[2,1]{0,1:T(1,128)}, u32[]{:S(2)}) copy-start(s32[2,1]{0,1:T(1,128)} %param.11) | copy-start | bytes 28
  8.1 7.6 %copy-start.5 = (f32[3072,128]{1,0:T(8,128)S(1)}, f32[3072,128]{1,0:T(8,128)}, u32[]{:S(2)}) copy-start(f32[3072,128]{1,0:T(8,128)} %param.6) | copy-start | bytes 4718596
  15.3 28.5 %collective-permute-start.1 = (f32[1024,128]{1,0:T(8,128)}, f32[1024,128]{1,0:T(8,128)}, u32[]{:S(2)}, u32[]{:S(2)}) collective-permute-start(f32[1024,128]{1,0:T(8,128)} %slice_bitcast_fusion.1), channel_id=1, source_target_pairs={{0,16},{16,0},{8,24},{24,8},{1,17},{17,1},{9,25},{25,9},{2,18},{18... | collective-permute-start | bytes 1572872 | tf_op jit(solution)/shard_map/ppermute | solution.py:198
  29.4 147.2 %all-gather.3.cloned.1.call-start = ((), (), s32[]{:S(2)}) async-start(), calls=%async_computation | async-start | bytes 14155776 | tf_op jit(solution)/shard_map/all_gather | solution.py:228
  29.5 14.3 %collective-permute-start = (s32[1024]{0:T(1024)S(1)}, s32[1024]{0:T(1024)S(1)}, u32[]{:S(2)}, u32[]{:S(2)}) collective-permute-start(s32[1024]{0:T(1024)S(1)} %bitcast.32), channel_id=1, source_target_pairs={{0,16},{16,0},{8,24},{24,8},{1,17},{17,1},{9,25},{25,9},{2,18},{18... | collective-permute-start | bytes 12296 | tf_op jit(solution)/shard_map/ppermute | solution.py:198
  52.4 127.6 %all-gather.5.cloned.1.call-start = ((), (), s32[]{:S(2)}) async-start(), calls=%async_computation.2 | async-start | bytes 4718592 | tf_op jit(solution)/shard_map/all_gather | solution.py:222
  71.2 230.5 %all-reduce.5.cloned.1.call-start = ((), (), s32[]{:S(2)}) async-start(), calls=%async_computation.3 | async-start | bytes 4194304 | tf_op jit(solution)/shard_map/psum | solution.py:238
  74.4 90.3 %collective-permute-start.2 = (f32[1024,512]{1,0:T(8,128)}, f32[1024,512]{1,0:T(8,128)S(1)}, u32[]{:S(2)}, u32[]{:S(2)}) collective-permute-start(f32[1024,512]{1,0:T(8,128)} %slice_bitcast_fusion), channel_id=1, source_target_pairs={{0,16},{16,0},{8,24},{24,8},{1,17},{17,1},{9,25},{25,9},{2,18},{18... | collective-permute-start | bytes 6291464 | tf_op jit(solution)/shard_map/ppermute | solution.py:198
  180.0 2.2 copy-start.4
  273.2 2.0 copy-start
  275.1 2.0 copy-start.3
  301.8 9.6 %copy-start.1 = (f32[1024,1024]{1,0:T(8,128)S(1)}, f32[1024,1024]{1,0:T(8,128)}, u32[]{:S(2)}) copy-start(f32[1024,1024]{1,0:T(8,128)} %copy-done) | copy-start | bytes 12582916
  318.2 1.6 copy-start.2
Sparse Core Ops, SparseCore 0:
  29.6 41.5 all-reduce.2
  180.1 88.4 all-reduce.4
Sparse Core Ops, SparseCore 1:
  52.5 78.0 all-gather.2
  132.3 37.1 all-gather.4

commit v2 on v1

--- a/solution.py
+++ b/solution.py
@@ -63,14 +63,19 @@
 
 
 def cholesky_kernel(diag_ref, upper_ref, inverse_ref):
-    size = diag_ref.shape[0]
+    pieces, size, narrow = diag_ref.shape
     count = size // TILE
+    per = TILE // narrow
+
+    def tile(i, j):
+        rows = slice(TILE * i, TILE * (i + 1))
+        parts = [diag_ref[piece, rows, :] for piece in range(per * j, per * (j + 1))]
+        return parts[0] if per == 1 else jnp.concatenate(parts, axis=1)
+
     for i in range(count):
         for j in range(i, count):
-            here = diag_ref[TILE * i : TILE * (i + 1), TILE * j : TILE * (j + 1)]
-            there = diag_ref[TILE * j : TILE * (j + 1), TILE * i : TILE * (i + 1)]
             inverse_ref[TILE * i : TILE * (i + 1), TILE * j : TILE * (j + 1)] = 0.5 * (
-                here + there.T
+                tile(i, j) + tile(j, i).T
             )
         if i:
             inverse_ref[TILE * i : TILE * (i + 1), : TILE * i] = jnp.zeros(
@@ -102,7 +107,7 @@
 
 
 def cholesky(diag):
-    size = diag.shape[0]
+    size = diag.shape[1]
     shape = jax.ShapeDtypeStruct((size, size), jnp.float32)
     return pl.pallas_call(
         cholesky_kernel,
@@ -122,70 +127,99 @@
     return high, (value - high.astype(jnp.float32)).astype(jnp.bfloat16)
 
 
+def dot_split(dims, left, right):
+    def dot(x, y):
+        return lax.dot_general(x, y, (dims, ((), ())), preferred_element_type=jnp.float32)
+
+    return (dot(left[0], right[1]) + dot(left[1], right[0])) + dot(left[0], right[0])
+
+
+def joined(ref):
+    return jnp.concatenate([ref[piece] for piece in range(ref.shape[0])], axis=1)
+
+
 def update_kernel(
-    top_tiles, root_ref, panel_ref, right_ref, trail_ref, window_ref, lower_ref,
-    factor_ref, schur_ref, high_ref, low_ref,
+    top_tiles, place_ref, panel_ref, inverse_ref, window_ref, upper_ref, trail_ref,
+    factor_ref, schur_ref, high_ref, low_ref, flipped_ref, first_ref,
 ):
     step = pl.program_id(0)
-    width = trail_ref.shape[1]
+    depth = inverse_ref.shape[0]
+    size, width = trail_ref.shape
+    narrow = upper_ref.shape[0]
+    at_root = place_ref[0] == 1
+    part = 256
 
     @pl.when(step == 0)
     def _():
-        high, low = halves(right_ref[...])
-        high_ref[...] = high
-        low_ref[...] = low
-
-    in_top = jnp.logical_and(root_ref[0] == 1, step < top_tiles)
+        window = joined(window_ref)
+        window_halves = halves(window)
+        for i in range(0, depth, part):
+            end = i + part
+            first_ref[i:end, :] = dot_split(
+                ((1,), (1,)),
+                halves(inverse_ref[i:end, :end]),
+                tuple(half[:, :end] for half in window_halves),
+            )
+        for i in range(0, depth, part):
+            second = dot_split(
+                ((0,), (0,)), halves(inverse_ref[i:, i : i + part]), halves(first_ref[i:, :])
+            )
+            high_ref[i : i + part, :width], low_ref[i : i + part, :width] = halves(second)
+        own = pl.ds(pl.multiple_of(place_ref[1] * narrow, narrow), narrow)
+        high_ref[:, width:], low_ref[:, width:] = halves(inverse_ref[own, :].T)
+
+        @pl.when(at_root)
+        def _():
+            flipped_ref[...] = window.T
+
+    in_top = jnp.logical_and(at_root, step < top_tiles)
 
     @pl.when(in_top)
     def _():
-        factor_ref[...] = lower_ref[...]
-        schur_ref[...] = trail_ref[...] - window_ref[...]
+        rows = pl.ds(pl.multiple_of(step * size, size), size)
+        factor_ref[...] = upper_ref[:, rows].T
+        schur_ref[...] = trail_ref[...] - flipped_ref[rows, :]
 
     @pl.when(jnp.logical_not(in_top))
     def _():
-        high, low = halves(panel_ref[...])
-        product = (
-            dot_nn(high, low_ref[...], None) + dot_nn(low, high_ref[...], None)
-        ) + dot_nn(high, high_ref[...], None)
+        product = dot_split(
+            ((1,), (0,)), halves(joined(panel_ref)), (high_ref[...], low_ref[...])
+        )
         factor_ref[...] = product[:, width:]
         schur_ref[...] = trail_ref[...] - product[:, :width]
 
 
-def update(root, panel, right, trail, window, lower):
-    rows, depth = panel.shape
-    width, narrow = trail.shape[1], lower.shape[1]
+def update(place, panel, inverse, window, upper, trail):
+    pieces, rows, narrow = panel.shape
+    depth = inverse.shape[0]
+    width = trail.shape[1]
     size = 512
-    top_tiles = depth // size
-
-    def capped(i, root):
-        return jnp.minimum(i, top_tiles - 1), 0
-
     return pl.pallas_call(
-        functools.partial(update_kernel, top_tiles),
+        functools.partial(update_kernel, depth // size),
         grid_spec=pltpu.PrefetchScalarGridSpec(
             num_scalar_prefetch=1,
             grid=(rows // size,),
             in_specs=[
-                pl.BlockSpec((size, depth), lambda i, root: (i, 0)),
-                pl.BlockSpec((depth, width + narrow), lambda i, root: (0, 0)),
-                pl.BlockSpec((size, width), lambda i, root: (i, 0)),
-                pl.BlockSpec((size, width), capped),
-                pl.BlockSpec((size, narrow), capped),
+                pl.BlockSpec((pieces, size, narrow), lambda i, place: (0, i, 0)),
+                pl.BlockSpec((depth, depth), lambda i, place: (0, 0)),
+                pl.BlockSpec((pieces, width, narrow), lambda i, place: (0, 0, 0)),
+                pl.BlockSpec((narrow, depth), lambda i, place: (place[1], 0)),
+                pl.BlockSpec((size, width), lambda i, place: (i, 0)),
             ],
             out_specs=(
-                pl.BlockSpec((size, narrow), lambda i, root: (i, 0)),
-                pl.BlockSpec((size, width), lambda i, root: (i, 0)),
+                pl.BlockSpec((size, narrow), lambda i, place: (i, 0)),
+                pl.BlockSpec((size, width), lambda i, place: (i, 0)),
             ),
-            scratch_shapes=[pltpu.VMEM((depth, width + narrow), jnp.bfloat16)] * 2,
+            scratch_shapes=[pltpu.VMEM((depth, width + narrow), jnp.bfloat16)] * 2
+            + [pltpu.VMEM((depth, width), jnp.float32)] * 2,
         ),
         out_shape=(
             jax.ShapeDtypeStruct((rows, narrow), jnp.float32),
             jax.ShapeDtypeStruct((rows, width), jnp.float32),
         ),
-        compiler_params=pltpu.CompilerParams(vmem_limit_bytes=48 << 20),
+        compiler_params=pltpu.CompilerParams(vmem_limit_bytes=56 << 20),
         name="factor_and_schur",
-    )(root, panel, right, trail, window, lower)
+    )(place, panel, inverse, window, upper, trail)
 
 
 def swapped(block, axis, distance):
@@ -219,32 +253,35 @@
         jnp.where(row_id == 1 << top_bit, partner_top, 0.0),
     )
     diag_piece = lax.psum(share, "row")
-    diag_full = lax.all_gather(diag_piece, "col", axis=1, tiled=True)
+    diag_full = lax.all_gather(diag_piece, "col", axis=0)
 
     partner_targets = swapped(targets[1], "row", top_bit)
     panel_slab = swapped(child_panel[1], "row", top_bit)
-    trail_slab = swapped(child_trail[1], "row", top_bit)
     panel = own_panel.at[partner_targets].add(panel_slab, mode="drop")
-    panel_full = lax.all_gather(panel, "col", axis=1, tiled=True)
+    sibling, _ = lax.optimization_barrier((child_trail[1], panel_slab))
+    trail_slab = swapped(sibling, "row", top_bit)
     trail = front_trail.at[targets[0]].add(child_trail[0], mode="drop")
+
+    window_rows = trail_cols * lax.axis_size("col")
+    blank = jnp.zeros((window_rows, panel_cols), jnp.float32)
+    window = lax.dynamic_slice_in_dim(
+        jnp.concatenate([blank, panel, blank], axis=0),
+        jnp.maximum(window_rows + panel_width - row_id * block_rows, 0),
+        window_rows,
+        0,
+    ).reshape(-1, trail_cols, panel_cols)
+    window = lax.all_to_all(window, "col", 0, 0)
+    window, _ = lax.optimization_barrier((window, diag_piece))
+    window = lax.psum(window, "row")
+
+    panel, _ = lax.optimization_barrier((panel, diag_full))
+    panel_full = lax.all_gather(panel, "col", axis=0)
+
+    upper, inverse = cholesky(diag_full)
+    trail_slab, _ = lax.optimization_barrier((trail_slab, inverse))
     trail = trail.at[partner_targets].add(trail_slab, mode="drop")
-
-    window_start = panel_width + col_id * trail_cols
-    window_root = window_start // block_rows
-    window_rows = lax.dynamic_slice_in_dim(
-        panel_full, window_start - window_root * block_rows, trail_cols, 0
-    )
-    window_rows, _ = lax.optimization_barrier((window_rows, diag_piece))
-    window = lax.psum(jnp.where(row_id == window_root, window_rows, 0.0), "row")
-
-    upper, inverse = cholesky(diag_full)
-    first = dot_nt(inverse, window)
-    second = dot_tn(inverse, first)
-    own_inverse = lax.dynamic_slice_in_dim(inverse, col_id * panel_cols, panel_cols, 0)
-    own_upper = lax.dynamic_slice_in_dim(upper, col_id * panel_cols, panel_cols, 0)
-    right = jnp.concatenate([second, own_inverse.T], axis=1)
-    root = (row_id == 0).astype(jnp.int32)[None]
-    return update(root, panel_full, right, trail, window.T, own_upper.T)
+    place = jnp.stack([(row_id == 0).astype(jnp.int32), col_id.astype(jnp.int32)])
+    return update(place, panel_full, inverse, window, upper, trail)
 
 
 def solution(mesh):

time: 350 us -> 396 us (1.13)
  waiting for transfers between devices: 107 us -> 168 us
  local copies, waits for them, and re-layouts: 45.8 us -> 12.4 us
  blocking collectives: 0 us -> 29.2 us
  matrix products: 16.4 us -> 0 us
  Pallas kernels: 110 us -> 117 us
    all_gather x2, waiting for transfers between devices: 0.03 us -> 57.8 us  [the longest x1 57.8 us: on_device(): panel_full = lax.all_gather(panel, 'col', axis=0)]
    all_to_all x0 -> x1, blocking collectives: none -> 29.2 us  [on_device(): window = lax.all_to_all(window, 'col', 0, 0)]
    psum x1, waiting for transfers between devices: 18.7 us -> 39.1 us  [on_device(): diag_piece = lax.psum(share, 'row')]
    ppermute x3, waiting for transfers between devices: 88.2 us -> 70.2 us  [swapped(): return lax.ppermute(block, axis, route)]
    dot_general x2 -> x0, matrix products: 16.4 us -> none  [the longest x1 9.64 us: dot_nt(): lax.dot_general(a, b, (((1,), (1,)), ((), ())), precision=precision, pref...]
    all_gather x1 -> x0, local copies, waits for them, and re-layouts: 12.6 us -> none  [on_device(): panel_full = lax.all_gather(panel, 'col', axis=1, tiled=True)]
    pallas_call x2 -> x0, local copies, waits for them, and re-layouts: 10.7 us -> none  [cholesky(): pl.pallas_call(cholesky_kernel, out_shape=(shape, shape), in_specs=[pl.Bl...]
    pallas_call x1, Pallas kernels: 19.3 us -> 25.9 us  [update(): pl.pallas_call(functools.partial(update_kernel, depth // size), grid_spec...]
  transfers between devices with their start and end apart: 7 -> 7, of which waited for: 3 -> 4; matrix products, arithmetic and copies ran while one was open for 23% -> 9% of each run, Pallas kernels for 26% -> 23%
where the time goes in v2:
time: 396 us; the launch traced here: 395 us
  waiting for transfers between devices  168 us (42%)
  Pallas kernels  117 us (30%)
  other arithmetic  48 us (12%)
  blocking collectives  29.2 us (7%)
  between operations  13.9 us (4%)
  local copies, waits for them, and re-layouts  12.4 us (3%)
  starting transfers between devices  6.77 us (2%)
    pallas_call x1, Pallas kernels, cholesky(): pl.pallas_call(cholesky_kernel, out_shape=(shape, shape), in_specs=[pl.Bl...  90.9 us
    ppermute x3, waiting for transfers between devices, swapped(): return lax.ppermute(block, axis, route)  70.2 us
    all_gather x1, waiting for transfers between devices, on_device(): panel_full = lax.all_gather(panel, 'col', axis=0)  57.8 us
    psum x1, waiting for transfers between devices, on_device(): diag_piece = lax.psum(share, 'row')  39.1 us
    all_to_all x1, blocking collectives, on_device(): window = lax.all_to_all(window, 'col', 0, 0)  29.2 us
    pallas_call x1, Pallas kernels, update(): pl.pallas_call(functools.partial(update_kernel, depth // size), grid_spec...  25.9 us
    scatter-add x1, other arithmetic, on_device(): trail = front_trail.at[targets[0]].add(child_trail[0], mode='drop')  12.7 us
    scatter-add x1, other arithmetic, on_device(): trail = trail.at[partner_targets].add(trail_slab, mode='drop')  11.9 us
  transfers between devices with their start and end apart: 7, of which 4 were waited for; matrix products, arithmetic and copies ran while one was open for 9% of the time, Pallas kernels for 23%

profile of v2, /device:TPU:20, one launch (start us, length us, event | category | flops | bytes accessed | tf_op | source)
XLA Modules:
  0.0 394.7 jit_solution(12540439418372533566)
XLA Ops:
  7.2 0.0 all-reduce.3.cloned.1.call-start
  7.2 0.0 copy-start.6
  7.2 0.0 copy-start.7
  7.2 0.0 copy-start.4
  7.2 0.0 copy-start.5
  7.3 6.2 %copy.17 = f32[3072,512]{1,0:T(8,128)} copy(f32[3072,512]{1,0:T(8,128)} %param.7) | data formatting | bytes 12582912
  13.5 0.0 copy-done.6
  13.5 0.0 copy-done.7
  13.5 0.1 compare_select_fusion.2
  13.6 0.0 copy-done.4
  13.6 0.0 copy-done.5
  13.6 6.7 %scatter_custom_fusion = f32[3072,128]{1,0:T(8,128)S(1)} fusion(f32[3072,128]{1,0:T(8,128)S(1)} %copy-done.4, s32[1024]{0:T(1024)S(1)} %bitcast.30, f32[2,1024,128]{2,1,0:T(8,128)S(1)} %copy-done.5), kind=kCustom, calls=%fused_computation.15 | custom fusion | flops 131072 | bytes 2097152 | tf_op jit(solution)/shard_map/scatter-add | solution.py:246
  20.3 6.2 %scatter_custom_fusion.2 = f32[1024,128]{1,0:T(8,128)S(1)} fusion(s32[1024]{0:T(1024)S(1)} %bitcast.32, f32[]{:T(128)} %constant.13.clone.1, f32[2,1024,128]{2,1,0:T(8,128)S(1)} %copy-done.5), kind=kCustom, calls=%fused_computation.19 | custom fusion | flops 131072 | bytes 1048580 | tf_op jit(solution)/shard_map/scatter-add | solution.py:247
  26.5 0.9 slice_select_fusion
  27.3 0.0 all-reduce.3.cloned.1.call-update
  27.3 0.0 all-gather.5.cloned.1.call-start
  27.4 39.1 %all-reduce.3.cloned.1.call-done = f32[1024,128]{1,0:T(8,128)} async-done(((f32[1024,128]{1,0:T(8,128)}), f32[1024,128]{1,0:T(8,128)}) %all-reduce.3.cloned.1.call-update) | async-done | bytes 524304 | tf_op jit(solution)/shard_map/psum | solution.py:255
  66.5 0.0 all-gather.5.cloned.1.call-update
  66.5 0.0 all-reduce.5.cloned.1.call-start
  66.6 0.9 collective-permute-start.1
  67.5 2.1 collective-permute-start
  69.6 19.8 %collective-permute-done = s32[1024]{0:T(1024)S(1)} collective-permute-done((s32[1024]{0:T(1024)S(1)}, s32[1024]{0:T(1024)S(1)}, u32[]{:S(2)}, u32[]{:S(2)}) %collective-permute-start) | collective-permute-done | bytes 4128 | tf_op jit(solution)/shard_map/ppermute | solution.py:232
  89.4 0.0 collective-permute-done.1
  89.4 6.6 %scatter_fusion = f32[3072,128]{1,0:T(8,128)S(1)} fusion(f32[3072,128]{1,0:T(8,128)S(1)} %scatter_custom_fusion, s32[1024]{0:T(1024)S(1)} %compare_select_fusion.3, f32[1024,128]{1,0:T(8,128)S(1)} %collective-permute-done.1), kind=kCustom, calls=%fused_computation.1 | custom fusion | flops 131072 | bytes 1576960 | tf_op jit(solution)/shard_map/scatter-add | solution.py:260
  96.0 0.0 copy-start.3
  96.0 0.1 broadcast_in_dim.23
  96.2 2.3 fusion.1
  98.5 0.0 copy-done.3
  98.5 29.2 %all_to_all.5 = f32[8,512,128]{2,1,0:T(8,128)} all-to-all(f32[8,512,128]{2,1,0:T(8,128)S(1)} %bitcast.28), channel_id=1, replica_groups=mesh['row'=4,'col'=8] {'col'}, dimensions={0} | all-to-all | bytes 4194304 | tf_op jit(solution)/shard_map/all_to_all | solution.py:273
  127.7 0.0 all-reduce.5.cloned.1.call-update
  127.8 0.0 all-gather.7.cloned.1.call-start
  127.8 0.0 all-gather.5.cloned.1.call-done
  127.8 0.5 all-gather.7.cloned.1.call-update
  128.3 12.7 %scatter_custom_fusion.3 = f32[3072,512]{1,0:T(8,128)} fusion(f32[3072,512]{1,0:T(8,128)} %copy.17, s32[1024]{0:T(1024)S(1)} %bitcast.31, f32[2,1024,512]{2,1,0:T(8,128)} %param.9), kind=kCustom, calls=%fused_computation.10 | custom fusion | flops 524288 | bytes 8388608 | tf_op jit(solution)/shard_map/scatter-add | solution.py:263
  141.1 0.7 pad_add_fusion.place_ref
  141.7 0.0 copy-start.2
  141.7 1.9 slice_bitcast_fusion
  143.6 3.6 collective-permute-start.2
  147.3 0.0 copy-done.2
  147.3 90.9 %cholesky_and_inverse.1 = (f32[1024,1024]{1,0:T(8,128)S(1)}, f32[1024,1024]{1,0:T(8,128)S(1)}) custom-call(f32[8,1024,128]{2,1,0:T(8,128)S(1)} %bitcast.26), custom_call_target="tpu_custom_call" | custom-call | flops 60000002048 | bytes 12582912 | tf_op jit(solution)/shard_map/cholesky_and_inverse/pallas_call | solution.py:112
  238.2 0.0 copy-start
  238.2 2.0 copy-done
  240.2 0.0 copy-start.1
  240.2 2.0 copy-done.1
  242.2 50.3 %collective-permute-done.2 = f32[1024,512]{1,0:T(8,128)S(1)} collective-permute-done((f32[1024,512]{1,0:T(8,128)S(1)}, f32[1024,512]{1,0:T(8,128)S(1)}, u32[]{:S(2)}, u32[]{:S(2)}) %collective-permute-start.2) | collective-permute-done | bytes 2097184 | tf_op jit(solution)/shard_map/ppermute | solution.py:232
  292.6 11.9 %scatter_fusion.1 = f32[3072,512]{1,0:T(8,128)} fusion(f32[3072,512]{1,0:T(8,128)} %scatter_custom_fusion.3, s32[1024]{0:T(1024)S(1)} %compare_select_fusion.3, f32[1024,512]{1,0:T(8,128)S(1)} %collective-permute-done.2), kind=kCustom, calls=%fused_computation.4 | custom fusion | flops 524288 | bytes 6295552 | tf_op jit(solution)/shard_map/scatter-add | solution.py:282
  304.5 57.8 %all-gather.7.cloned.1.call-done = f32[24576,128]{1,0:T(8,128)} async-done(((f32[3072,128]{1,0:T(8,128)}), f32[24576,128]{1,0:T(8,128)}) %all-gather.7.cloned.1.call-update) | async-done | bytes 12582928 | tf_op jit(solution)/shard_map/all_gather | solution.py:278
  362.2 25.9 %factor_and_schur.1 = (f32[3072,128]{1,0:T(8,128)}, f32[3072,512]{1,0:T(8,128)}) custom-call(s32[2]{0:T(128)} %pad_add_fusion.place_ref, f32[8,3072,128]{2,1,0:T(8,128)} %bitcast.27, f32[1024,1024]{1,0:T(8,128)} %copy-done.1, f32[8,512,128]{2,1,0:T(8,128)} %all-reduce.5.cloned.1.call-done.window_ref, f32[1024,1024]{1,0:T(8,128)} %copy-done, ...), custom_call_target="tpu_custom_call" | custom-call | tf_op jit(solution)/shard_map/factor_and_schur/pallas_call | solution.py:197
  (5 shorter events, 0.1 us)
Async XLA Ops:
  7.2 59.3 %all-reduce.3.cloned.1.call-start = ((), (), s32[]{:S(2)}) async-start(), calls=%async_computation.1 | async-start | bytes 1048576 | tf_op jit(solution)/shard_map/psum | solution.py:255
  7.2 6.3 %copy-start.6 = (s32[2,1024]{1,0:T(2,128)S(1)}, s32[2,1024]{1,0:T(2,128)}, u32[]{:S(2)}) copy-start(s32[2,1024]{1,0:T(2,128)} %param.10) | copy-start | bytes 24580
  7.2 6.3 %copy-start.7 = (s32[2,1]{0,1:T(1,128)S(1)}, s32[2,1]{0,1:T(1,128)}, u32[]{:S(2)}) copy-start(s32[2,1]{0,1:T(1,128)} %param.11) | copy-start | bytes 28
  7.2 6.4 %copy-start.4 = (f32[3072,128]{1,0:T(8,128)S(1)}, f32[3072,128]{1,0:T(8,128)}, u32[]{:S(2)}) copy-start(f32[3072,128]{1,0:T(8,128)} %param.6) | copy-start | bytes 4718596
  7.2 6.4 %copy-start.5 = (f32[2,1024,128]{2,1,0:T(8,128)S(1)}, f32[2,1024,128]{2,1,0:T(8,128)}, u32[]{:S(2)}) copy-start(f32[2,1024,128]{2,1,0:T(8,128)} %param.8) | copy-start | bytes 3145732
  27.3 100.5 %all-gather.5.cloned.1.call-start = ((), (), s32[]{:S(2)}) async-start(), calls=%async_computation.3 | async-start | bytes 4718592 | tf_op jit(solution)/shard_map/all_gather | solution.py:256
  66.5 238.0 %all-reduce.5.cloned.1.call-start = ((), (), s32[]{:S(2)}) async-start(), calls=%async_computation.2 | async-start | bytes 4194304 | tf_op jit(solution)/shard_map/psum | solution.py:275
  66.6 22.8 %collective-permute-start.1 = (f32[1024,128]{1,0:T(8,128)S(1)}, f32[1024,128]{1,0:T(8,128)S(1)}, u32[]{:S(2)}, u32[]{:S(2)}) collective-permute-start(f32[1024,128]{1,0:T(8,128)S(1)} %slice_bitcast_fusion.1), channel_id=1, source_target_pairs={{0,16},{16,0},{8,24},{24,8},{1,17},{17,1},{9,25},{25,9},{2,18},{18... | collective-permute-start | bytes 1572872 | tf_op jit(solution)/shard_map/ppermute | solution.py:232
  67.5 21.9 %collective-permute-start = (s32[1024]{0:T(1024)S(1)}, s32[1024]{0:T(1024)S(1)}, u32[]{:S(2)}, u32[]{:S(2)}) collective-permute-start(s32[1024]{0:T(1024)S(1)} %bitcast.29), channel_id=1, source_target_pairs={{0,16},{16,0},{8,24},{24,8},{1,17},{17,1},{9,25},{25,9},{2,18},{18... | collective-permute-start | bytes 12296 | tf_op jit(solution)/shard_map/ppermute | solution.py:232
  96.0 2.5 copy-start.3
  127.8 234.5 %all-gather.7.cloned.1.call-start = ((), (), s32[]{:S(2)}) async-start(), calls=%async_computation.4 | async-start | bytes 14155776 | tf_op jit(solution)/shard_map/all_gather | solution.py:278
  141.7 5.5 %copy-start.2 = (f32[8192,128]{1,0:T(8,128)S(1)}, f32[8192,128]{1,0:T(8,128)}, u32[]{:S(2)}) copy-start(f32[8192,128]{1,0:T(8,128)} %all-gather.5.cloned.1.call-done) | copy-start | bytes 12582916
  143.6 148.9 %collective-permute-start.2 = (f32[1024,512]{1,0:T(8,128)S(1)}, f32[1024,512]{1,0:T(8,128)S(1)}, u32[]{:S(2)}, u32[]{:S(2)}) collective-permute-start(f32[1024,512]{1,0:T(8,128)S(1)} %slice_bitcast_fusion), channel_id=1, source_target_pairs={{0,16},{16,0},{8,24},{24,8},{1,17},{17,1},{9,25},{25,9},{2,18},{18... | collective-permute-start | bytes 6291464 | tf_op jit(solution)/shard_map/ppermute | solution.py:232
  238.2 2.0 copy-start
  240.2 2.0 copy-start.1
Sparse Core Ops, SparseCore 0:
  27.5 38.9 all-reduce.2
  68.3 36.8 all-gather.4
  127.9 158.4 all-reduce.4
  288.9 73.3 all-gather.6

commit v3 on v2

--- a/solution.py
+++ b/solution.py
@@ -9,7 +9,7 @@
 
 HIGHEST = lax.Precision.HIGHEST
 TILE = 128
-GROUP = 8
+GROUP = 16
 
 
 def dot_tn(a, b, precision=HIGHEST):
@@ -62,7 +62,35 @@
     return jnp.concatenate(left, axis=0), jnp.concatenate(right, axis=0)
 
 
-def cholesky_kernel(diag_ref, upper_ref, inverse_ref):
+def eliminate(first, last, upper_ref, inverse_ref):
+    size = inverse_ref.shape[0]
+    count = size // TILE
+    block = lax.broadcasted_iota(jnp.int32, (TILE, size), 1) // TILE
+
+    def step(b, carry):
+        at = pl.multiple_of(b * TILE, TILE)
+        rows, cols = pl.ds(at, TILE), pl.ds(at, TILE)
+        top, inv = factor_tile(inverse_ref[rows, cols])
+        scaled = dot_nn(inv, inverse_ref[rows, :])
+        upper_ref[rows, :] = jnp.where(block > b, scaled, 0.0)
+        upper_ref[rows, cols] = top
+        inverse_ref[rows, :] = scaled
+        inverse_ref[rows, cols] = inv
+
+        def below(s, inner):
+            under = pl.ds(pl.multiple_of(s * TILE, TILE), TILE)
+            change = dot_tn(upper_ref[rows, under], inverse_ref[rows, :])
+            inverse_ref[under, :] = jnp.where(block == b, 0.0, inverse_ref[under, :]) - change
+            return inner
+
+        lax.fori_loop(b + 1, count, below, 0)
+        inverse_ref[rows, :] = jnp.where(block <= b, inverse_ref[rows, :], 0.0)
+        return carry
+
+    lax.fori_loop(first, last, step, 0)
+
+
+def first_kernel(last, diag_ref, upper_ref, inverse_ref):
     pieces, size, narrow = diag_ref.shape
     count = size // TILE
     per = TILE // narrow
@@ -81,45 +109,35 @@
             inverse_ref[TILE * i : TILE * (i + 1), : TILE * i] = jnp.zeros(
                 (TILE, TILE * i), jnp.float32
             )
-    block = lax.broadcasted_iota(jnp.int32, (TILE, size), 1) // TILE
-
-    def step(b, carry):
-        at = pl.multiple_of(b * TILE, TILE)
-        rows, cols = pl.ds(at, TILE), pl.ds(at, TILE)
-        top, inv = factor_tile(inverse_ref[rows, cols])
-        scaled = dot_nn(inv, inverse_ref[rows, :])
-        upper_ref[rows, :] = jnp.where(block > b, scaled, 0.0)
-        upper_ref[rows, cols] = top
-        inverse_ref[rows, :] = scaled
-        inverse_ref[rows, cols] = inv
-
-        def below(s, inner):
-            under = pl.ds(pl.multiple_of(s * TILE, TILE), TILE)
-            change = dot_tn(upper_ref[rows, under], inverse_ref[rows, :])
-            inverse_ref[under, :] = jnp.where(block == b, 0.0, inverse_ref[under, :]) - change
-            return inner
-
-        lax.fori_loop(b + 1, count, below, 0)
-        inverse_ref[rows, :] = jnp.where(block <= b, inverse_ref[rows, :], 0.0)
-        return carry
-
-    lax.fori_loop(0, count, step, 0)
-
-
-def cholesky(diag):
-    size = diag.shape[1]
+    eliminate(0, last, upper_ref, inverse_ref)
+
+
+def next_kernel(first, last, upper_in, inverse_in, upper_ref, inverse_ref):
+    upper_ref[...] = upper_in[...]
+    inverse_ref[...] = inverse_in[...]
+    eliminate(first, last, upper_ref, inverse_ref)
+
+
+def cholesky_part(first, last, *operands):
+    size = operands[0].shape[-2]
     shape = jax.ShapeDtypeStruct((size, size), jnp.float32)
+    if first:
+        kernel = functools.partial(next_kernel, first, last)
+    else:
+        kernel = functools.partial(first_kernel, last)
     return pl.pallas_call(
-        cholesky_kernel,
+        kernel,
         out_shape=(shape, shape),
-        in_specs=[pl.BlockSpec(memory_space=pltpu.VMEM)],
+        in_specs=[pl.BlockSpec(memory_space=pltpu.VMEM)] * len(operands),
         out_specs=(pl.BlockSpec(memory_space=pltpu.VMEM),) * 2,
         compiler_params=pltpu.CompilerParams(vmem_limit_bytes=40 << 20),
         cost_estimate=pl.CostEstimate(
-            flops=60_000_000_000, bytes_accessed=12 * size * size, transcendentals=0
+            flops=7_500_000_000 * (last - first),
+            bytes_accessed=12 * size * size,
+            transcendentals=0,
         ),
         name="cholesky_and_inverse",
-    )(diag)
+    )(*operands)
 
 
 def halves(value):
@@ -232,6 +250,18 @@
     return lax.ppermute(block, axis, route)
 
 
+def spread(level, panel_width, trail_cols, block_rows):
+    rows, cols = lax.axis_size("row"), lax.axis_size("col")
+    stride = rows >> level + 1
+    route = []
+    for col in range(cols):
+        root = (panel_width + col * trail_cols) // block_rows
+        for other in range(0, rows, 2 * stride):
+            here = root ^ other
+            route.append((here * cols + col, (here ^ stride) * cols + col))
+    return route
+
+
 def on_device(front_panel, front_trail, child_panel, child_trail, child_map, child_count):
     block_rows, panel_cols = front_panel.shape
     trail_cols = front_trail.shape[1]
@@ -253,14 +283,18 @@
         jnp.where(row_id == 1 << top_bit, partner_top, 0.0),
     )
     diag_piece = lax.psum(share, "row")
-    diag_full = lax.all_gather(diag_piece, "col", axis=0)
 
     partner_targets = swapped(targets[1], "row", top_bit)
     panel_slab = swapped(child_panel[1], "row", top_bit)
+    half = slab_rows // 2
+    early_slab = swapped(child_trail[1, :half], "row", top_bit)
+    late_slab = swapped(child_trail[1, half:], "row", top_bit)
     panel = own_panel.at[partner_targets].add(panel_slab, mode="drop")
-    sibling, _ = lax.optimization_barrier((child_trail[1], panel_slab))
-    trail_slab = swapped(sibling, "row", top_bit)
+    diag_piece, panel, early_slab = lax.optimization_barrier((diag_piece, panel, early_slab))
+    diag_full = lax.all_gather(diag_piece, "col", axis=0)
     trail = front_trail.at[targets[0]].add(child_trail[0], mode="drop")
+    trail = trail.at[partner_targets[:half]].add(early_slab, mode="drop")
+    trail = trail.at[partner_targets[half:]].add(late_slab, mode="drop")
 
     window_rows = trail_cols * lax.axis_size("col")
     blank = jnp.zeros((window_rows, panel_cols), jnp.float32)
@@ -271,15 +305,22 @@
         0,
     ).reshape(-1, trail_cols, panel_cols)
     window = lax.all_to_all(window, "col", 0, 0)
-    window, _ = lax.optimization_barrier((window, diag_piece))
-    window = lax.psum(window, "row")
-
-    panel, _ = lax.optimization_barrier((panel, diag_full))
+
+    diag_full, panel, window, trail = lax.optimization_barrier((diag_full, panel, window, trail))
     panel_full = lax.all_gather(panel, "col", axis=0)
 
-    upper, inverse = cholesky(diag_full)
-    trail_slab, _ = lax.optimization_barrier((trail_slab, inverse))
-    trail = trail.at[partner_targets].add(trail_slab, mode="drop")
+    count = panel_width // TILE
+    state = (diag_full,)
+    for level in range(top_bit + 1):
+        route = spread(level, panel_width, trail_cols, block_rows)
+        arrived = lax.ppermute(window, ("row", "col"), route)
+        first, last = (count * at // (top_bit + 1) for at in (level, level + 1))
+        state = cholesky_part(first, last, *state)
+        arrived, *state = lax.optimization_barrier((arrived, *state))
+        window = window + arrived
+        if level < top_bit:
+            window, *state = lax.optimization_barrier((window, *state))
+    upper, inverse = state
     place = jnp.stack([(row_id == 0).astype(jnp.int32), col_id.astype(jnp.int32)])
     return update(place, panel_full, inverse, window, upper, trail)
 

time: 396 us -> 313 us (0.79)
  waiting for transfers between devices: 168 us -> 123 us
  blocking collectives: 29.2 us -> 0 us
  Pallas kernels: 117 us -> 89.4 us
  other arithmetic: 48 us -> 58.4 us
  local copies, waits for them, and re-layouts: 12.4 us -> 16.8 us
  starting transfers between devices: 6.77 us -> 10.8 us
    all_gather x1, waiting for transfers between devices: 57.8 us -> 0.01 us  [on_device(): panel_full = lax.all_gather(panel, 'col', axis=0)]
    all_to_all x1 -> x0, blocking collectives: 29.2 us -> none  [on_device(): window = lax.all_to_all(window, 'col', 0, 0)]
    pallas_call x1 -> x2, Pallas kernels: 90.9 us -> 63.5 us  [cholesky_part(): pl.pallas_call(kernel, out_shape=(shape, shape), in_specs=[pl.BlockSpec(m...]
    ppermute x0 -> x2, waiting for transfers between devices: none -> 24.9 us  [on_device(): arrived = lax.ppermute(window, ('row', 'col'), route)]
    psum x1, waiting for transfers between devices: 39.1 us -> 17.4 us  [on_device(): diag_piece = lax.psum(share, 'row')]
    ppermute x3 -> x4, waiting for transfers between devices: 70.2 us -> 80.7 us  [swapped(): return lax.ppermute(block, axis, route)]
    scatter-add x1 -> x2, other arithmetic: 11.9 us -> 18.5 us  [the longest x1 9.57 us: on_device(): trail = trail.at[partner_targets[:half]].add(early_slab, mode='drop')]
    all_to_all x0 -> x1, starting transfers between devices: none -> 4.27 us  [on_device(): window = lax.all_to_all(window, 'col', 0, 0)]
  transfers between devices with their start and end apart: 7 -> 10, of which waited for: 4 -> 4; matrix products, arithmetic and copies ran while one was open for 9% -> 19% of each run, Pallas kernels for 23% -> 20%
where the time goes in v3:
time: 313 us; the launch traced here: 312 us
  waiting for transfers between devices  123 us (39%)
  Pallas kernels  89.4 us (29%)
  other arithmetic  58.4 us (19%)
  local copies, waits for them, and re-layouts  16.8 us (5%)
  between operations  13.9 us (4%)
  starting transfers between devices  10.8 us (3%)
    ppermute x4, waiting for transfers between devices, swapped(): return lax.ppermute(block, axis, route)  80.7 us
    pallas_call x2, Pallas kernels, cholesky_part(): pl.pallas_call(kernel, out_shape=(shape, shape), in_specs=[pl.BlockSpec(m...  63.5 us
    pallas_call x1, Pallas kernels, update(): pl.pallas_call(functools.partial(update_kernel, depth // size), grid_spec...  25.9 us
    ppermute x2, waiting for transfers between devices, on_device(): arrived = lax.ppermute(window, ('row', 'col'), route)  24.9 us
    psum x1, waiting for transfers between devices, on_device(): diag_piece = lax.psum(share, 'row')  17.4 us
    unnamed x21, local copies, waits for them, and re-layouts  14.3 us
    scatter-add x1, other arithmetic, on_device(): trail = front_trail.at[targets[0]].add(child_trail[0], mode='drop')  13.1 us
    scatter-add x1, other arithmetic, on_device(): trail = trail.at[partner_targets[:half]].add(early_slab, mode='drop')  9.57 us
  transfers between devices with their start and end apart: 10, of which 4 were waited for; matrix products, arithmetic and copies ran while one was open for 19% of the time, Pallas kernels for 20%

profile of v3, /device:TPU:20, one launch (start us, length us, event | category | flops | bytes accessed | tf_op | source)
XLA Modules:
  0.0 312.3 jit_solution(13930673542981467645)
XLA Ops:
  7.2 0.0 all-reduce.2.cloned.1.call-start
  7.2 0.0 copy-start.7
  7.2 0.0 copy-start.6
  7.2 6.3 %copy.17 = f32[3072,512]{1,0:T(8,128)} copy(f32[3072,512]{1,0:T(8,128)} %param.7) | data formatting | bytes 12582912
  13.5 0.8 slice_bitcast_fusion.2
  14.4 0.3 collective-permute-start.1
  14.7 1.5 slice_bitcast_fusion
  16.2 2.6 collective-permute-start.2
  18.8 0.1 compare_select_fusion.2
  18.9 6.7 %scatter_custom_fusion = f32[3072,128]{1,0:T(8,128)S(1)} fusion(f32[3072,128]{1,0:T(8,128)S(1)} %copy-done.5, s32[1024]{0:T(1024)S(1)} %bitcast.32, f32[2,1024,128]{2,1,0:T(8,128)S(1)} %copy-done.7), kind=kCustom, calls=%fused_computation.17 | custom fusion | flops 131072 | bytes 2097152 | tf_op jit(solution)/shard_map/scatter-add | solution.py:276
  25.5 6.2 %scatter_custom_fusion.1 = f32[1024,128]{1,0:T(8,128)S(1)} fusion(s32[1024]{0:T(1024)S(1)} %bitcast.34, f32[]{:T(128)} %constant.13.clone.1, f32[2,1024,128]{2,1,0:T(8,128)S(1)} %copy-done.7), kind=kCustom, calls=%fused_computation.21 | custom fusion | flops 131072 | bytes 1048580 | tf_op jit(solution)/shard_map/scatter-add | solution.py:277
  31.7 0.9 slice_select_fusion
  32.6 0.0 all-reduce.2.cloned.1.call-update
  32.6 0.0 all-gather.5.cloned.1.call-start
  32.7 0.4 collective-permute-start
  33.1 57.8 %collective-permute-done = s32[1024]{0:T(1024)S(1)} collective-permute-done((s32[1024]{0:T(1024)S(1)}, s32[1024]{0:T(1024)S(1)}, u32[]{:S(2)}, u32[]{:S(2)}) %collective-permute-start) | collective-permute-done | bytes 4128 | tf_op jit(solution)/shard_map/ppermute | solution.py:250
  90.9 0.0 collective-permute-done.1
  90.9 7.0 %scatter_fusion = f32[3072,128]{1,0:T(8,128)S(1)} fusion(f32[3072,128]{1,0:T(8,128)S(1)} %scatter_custom_fusion, s32[1024]{0:T(1024)S(1)} %compare_select_fusion.3, f32[1024,128]{1,0:T(8,128)} %collective-permute-done.1), kind=kCustom, calls=%fused_computation.2 | custom fusion | flops 131072 | bytes 1576960 | tf_op jit(solution)/shard_map/scatter-add | solution.py:292
  97.9 0.0 copy-start.4
  98.0 17.4 %all-reduce.2.cloned.1.call-done = f32[1024,128]{1,0:T(8,128)} async-done(((f32[1024,128]{1,0:T(8,128)}), f32[1024,128]{1,0:T(8,128)}) %all-reduce.2.cloned.1.call-update) | async-done | bytes 524304 | tf_op jit(solution)/shard_map/psum | solution.py:285
  115.3 0.0 collective-permute-done.2
  115.3 0.0 all-gather.5.cloned.1.call-update
  115.4 0.1 broadcast_in_dim.28
  115.5 3.6 %fusion.1 = f32[4096,128]{1,0:T(8,128)} fusion(s32[]{:T(128)S(6)} %max.3, f32[4096,128]{1,0:T(8,128)S(1)} %broadcast_in_dim.28, f32[3072,128]{1,0:T(8,128)S(1)} %scatter_fusion), kind=kLoop, calls=%fused_computation.10 | loop fusion | flops 1048576 | bytes 5767172 | tf_op jit(solution)/shard_map/concatenate | solution.py:302
  119.1 4.3 %all-to-all-start = ((f32[8,512,128]{2,1,0:T(8,128)}), f32[8,512,128]{2,1,0:T(8,128)S(1)}, u32[]{:S(2)}, u32[]{:S(2)}) async-start(f32[8,512,128]{2,1,0:T(8,128)} %bitcast.30), calls=%async_computation | async-start | bytes 4194304 | tf_op jit(solution)/shard_map/all_to_all | solution.py:307
  123.4 0.0 all-gather.7.cloned.1.call-start
  123.4 0.9 collective-permute-start.3
  124.3 13.1 %scatter_custom_fusion.3 = f32[3072,512]{1,0:T(8,128)} fusion(f32[3072,512]{1,0:T(8,128)} %copy.17, s32[1024]{0:T(1024)S(1)} %bitcast.33, f32[2,1024,512]{2,1,0:T(8,128)} %param.9), kind=kCustom, calls=%fused_computation.11 | custom fusion | flops 524288 | bytes 8388608 | tf_op jit(solution)/shard_map/scatter-add | solution.py:295
  137.4 9.6 %scatter_fusion.1 = f32[3072,512]{1,0:T(8,128)} fusion(f32[3072,512]{1,0:T(8,128)} %scatter_custom_fusion.3, s32[512]{0:T(512)S(1)} %get-tuple-element.47, f32[512,512]{1,0:T(8,128)} %collective-permute-done.2), kind=kCustom, calls=%fused_computation.4 | custom fusion | flops 262144 | bytes 3147776 | tf_op jit(solution)/shard_map/scatter-add | solution.py:296
  146.9 22.8 %collective-permute-done.3 = f32[512,512]{1,0:T(8,128)S(1)} collective-permute-done((f32[512,512]{1,0:T(8,128)}, f32[512,512]{1,0:T(8,128)S(1)}, u32[]{:S(2)}, u32[]{:S(2)}) %collective-permute-start.3) | collective-permute-done | bytes 1048608 | tf_op jit(solution)/shard_map/ppermute | solution.py:250
  169.8 8.9 %scatter_fusion.2 = f32[3072,512]{1,0:T(8,128)} fusion(f32[3072,512]{1,0:T(8,128)} %scatter_fusion.1, s32[512]{0:T(512)S(1)} %get-tuple-element.46, f32[512,512]{1,0:T(8,128)S(1)} %collective-permute-done.3), kind=kCustom, calls=%fused_computation.5 | custom fusion | flops 262144 | bytes 3147776 | tf_op jit(solution)/shard_map/scatter-add | solution.py:297
  178.7 0.0 all-to-all-done
  178.7 0.0 all-gather.7.cloned.1.call-update
  178.7 0.6 pad_add_fusion.place_ref
  179.3 0.8 collective-permute-start.4
  180.1 2.2 copy-done.2
  182.3 35.8 %cholesky_and_inverse.2 = (f32[1024,1024]{1,0:T(8,128)S(1)}, f32[1024,1024]{1,0:T(8,128)S(1)}) custom-call(f32[8,1024,128]{2,1,0:T(8,128)S(1)} %bitcast.28), custom_call_target="tpu_custom_call" | custom-call | flops 30000001024 | bytes 12582912 | tf_op jit(solution)/shard_map/cholesky_and_inverse/pallas_call | solution.py:128
  218.1 0.0 copy-start.3
  218.1 0.0 collective-permute-done.4
  218.1 0.2 add.60
  218.3 1.8 copy-done.3
  220.1 1.5 collective-permute-start.5
  221.6 27.8 %cholesky_and_inverse.3 = (f32[1024,1024]{1,0:T(8,128)S(1)}, f32[1024,1024]{1,0:T(8,128)S(1)}) custom-call(f32[1024,1024]{1,0:T(8,128)S(1)} %get-tuple-element.34.upper_in, f32[1024,1024]{1,0:T(8,128)} %copy-done.3), custom_call_target="tpu_custom_call" | custom-call | flops 30000001024 | bytes 12582912 | tf_op jit(solution)/shard_map/cholesky_and_inverse/pallas_call | solution.py:128
  249.4 2.0 copy-done
  251.4 2.0 copy-done.1
  253.4 24.9 %collective-permute-done.5 = f32[8,512,128]{2,1,0:T(8,128)S(1)} collective-permute-done((f32[8,512,128]{2,1,0:T(8,128)S(1)}, f32[8,512,128]{2,1,0:T(8,128)S(1)}, u32[]{:S(2)}, u32[]{:S(2)}) %collective-permute-start.5) | collective-permute-done | bytes 2097184 | tf_op jit(solution)/shard_map/ppermute | solution.py:316
  278.3 1.5 add.61.window_ref
  279.8 25.9 %factor_and_schur.1 = (f32[3072,128]{1,0:T(8,128)}, f32[3072,512]{1,0:T(8,128)}) custom-call(s32[2]{0:T(128)} %pad_add_fusion.place_ref, f32[8,3072,128]{2,1,0:T(8,128)} %bitcast.29, f32[1024,1024]{1,0:T(8,128)} %copy-done.1, f32[8,512,128]{2,1,0:T(8,128)} %add.61.window_ref, f32[1024,1024]{1,0:T(8,128)} %copy-done, f32[3072,512]{1,0:T(8,128)} %scatter_fusion.2), custom_call_target="tpu_custom_call" | custom-call | tf_op jit(solution)/shard_map/factor_and_schur/pallas_call | solution.py:215
  (18 shorter events, 0.1 us)
Async XLA Ops:
  7.2 108.2 %all-reduce.2.cloned.1.call-start = ((), (), s32[]{:S(2)}) async-start(), calls=%async_computation.1 | async-start | bytes 1048576 | tf_op jit(solution)/shard_map/psum | solution.py:285
  7.2 6.3 %copy-start.7 = (f32[2,1024,128]{2,1,0:T(8,128)S(1)}, f32[2,1024,128]{2,1,0:T(8,128)}, u32[]{:S(2)}) copy-start(f32[2,1024,128]{2,1,0:T(8,128)} %param.8) | copy-start | bytes 3145732
  7.2 7.5 %copy-start.6 = (f32[2,1024,512]{2,1,0:T(8,128)S(1)}, f32[2,1024,512]{2,1,0:T(8,128)}, u32[]{:S(2)}) copy-start(f32[2,1024,512]{2,1,0:T(8,128)} %param.9) | copy-start | bytes 12582916
  14.3 4.4 %copy-start.8 = (s32[2,1024]{1,0:T(2,128)S(1)}, s32[2,1024]{1,0:T(2,128)}, u32[]{:S(2)}) copy-start(s32[2,1024]{1,0:T(2,128)} %param.10) | copy-start | bytes 24580
  14.3 4.4 %copy-start.9 = (s32[2,1]{0,1:T(1,128)S(1)}, s32[2,1]{0,1:T(1,128)}, u32[]{:S(2)}) copy-start(s32[2,1]{0,1:T(1,128)} %param.11) | copy-start | bytes 28
  14.3 4.5 %copy-start.5 = (f32[3072,128]{1,0:T(8,128)S(1)}, f32[3072,128]{1,0:T(8,128)}, u32[]{:S(2)}) copy-start(f32[3072,128]{1,0:T(8,128)} %param.6) | copy-start | bytes 4718596
  14.4 76.6 %collective-permute-start.1 = (f32[1024,128]{1,0:T(8,128)}, f32[1024,128]{1,0:T(8,128)}, u32[]{:S(2)}, u32[]{:S(2)}) collective-permute-start(f32[1024,128]{1,0:T(8,128)} %slice_bitcast_fusion.2), channel_id=1, source_target_pairs={{0,16},{16,0},{8,24},{24,8},{1,17},{17,1},{9,25},{25,9},{2,18},{18... | collective-permute-start | bytes 1572872 | tf_op jit(solution)/shard_map/ppermute | solution.py:250
  16.2 99.1 %collective-permute-start.2 = (f32[512,512]{1,0:T(8,128)}, f32[512,512]{1,0:T(8,128)}, u32[]{:S(2)}, u32[]{:S(2)}) collective-permute-start(f32[512,512]{1,0:T(8,128)} %get-tuple-element.43), channel_id=1, source_target_pairs={{0,16},{16,0},{8,24},{24,8},{1,17},{17,1},{9,25},{25,9},{2,18},{18... | collective-permute-start | bytes 3145736 | tf_op jit(solution)/shard_map/ppermute | solution.py:250
  32.6 146.0 %all-gather.5.cloned.1.call-start = ((), (), s32[]{:S(2)}) async-start(), calls=%async_computation.2 | async-start | bytes 4718592 | tf_op jit(solution)/shard_map/all_gather | solution.py:294
  32.7 58.2 %collective-permute-start = (s32[1024]{0:T(1024)S(1)}, s32[1024]{0:T(1024)S(1)}, u32[]{:S(2)}, u32[]{:S(2)}) collective-permute-start(s32[1024]{0:T(1024)S(1)} %bitcast.31), channel_id=1, source_target_pairs={{0,16},{16,0},{8,24},{24,8},{1,17},{17,1},{9,25},{25,9},{2,18},{18... | collective-permute-start | bytes 12296 | tf_op jit(solution)/shard_map/ppermute | solution.py:250
  97.9 21.2 %copy-start.4 = (f32[3072,128]{1,0:T(8,128)}, f32[3072,128]{1,0:T(8,128)S(1)}, u32[]{:S(2)}) copy-start(f32[3072,128]{1,0:T(8,128)S(1)} %scatter_fusion) | copy-start | bytes 4718596
  119.1 59.5 %all-to-all-start = ((f32[8,512,128]{2,1,0:T(8,128)}), f32[8,512,128]{2,1,0:T(8,128)S(1)}, u32[]{:S(2)}, u32[]{:S(2)}) async-start(f32[8,512,128]{2,1,0:T(8,128)} %bitcast.30), calls=%async_computation | async-start | bytes 4194304 | tf_op jit(solution)/shard_map/all_to_all | solution.py:307
  123.4 156.4 %all-gather.7.cloned.1.call-start = ((), (), s32[]{:S(2)}) async-start(), calls=%async_computation.3 | async-start | bytes 14155776 | tf_op jit(solution)/shard_map/all_gather | solution.py:310
  123.4 46.4 %collective-permute-start.3 = (f32[512,512]{1,0:T(8,128)}, f32[512,512]{1,0:T(8,128)S(1)}, u32[]{:S(2)}, u32[]{:S(2)}) collective-permute-start(f32[512,512]{1,0:T(8,128)} %get-tuple-element.42), channel_id=1, source_target_pairs={{0,16},{16,0},{8,24},{24,8},{1,17},{17,1},{9,25},{25,9},{2,18},{18... | collective-permute-start | bytes 3145736 | tf_op jit(solution)/shard_map/ppermute | solution.py:250
  179.3 38.8 %collective-permute-start.4 = (f32[8,512,128]{2,1,0:T(8,128)S(1)}, f32[8,512,128]{2,1,0:T(8,128)S(1)}, u32[]{:S(2)}, u32[]{:S(2)}) collective-permute-start(f32[8,512,128]{2,1,0:T(8,128)S(1)} %all-to-all-done), channel_id=1, source_target_pairs={{0,16},{1,17},{2,18},{3,19},{12,28},{13,29},{14,30},{15,31}} | collective-permute-start | bytes 6291464 | tf_op jit(solution)/shard_map/ppermute | solution.py:316
  180.1 2.2 copy-start.2
  218.1 2.0 copy-start.3
  220.1 58.2 %collective-permute-start.5 = (f32[8,512,128]{2,1,0:T(8,128)S(1)}, f32[8,512,128]{2,1,0:T(8,128)S(1)}, u32[]{:S(2)}, u32[]{:S(2)}) collective-permute-start(f32[8,512,128]{2,1,0:T(8,128)S(1)} %add.60), channel_id=1, source_target_pairs={{0,8},{16,24},{1,9},{17,25},{2,10},{18,26},{3,11},{19,27},{12,4},{... | collective-permute-start | bytes 6291464 | tf_op jit(solution)/shard_map/ppermute | solution.py:316
  249.4 2.0 copy-start
  251.4 2.0 copy-start.1
Sparse Core Ops, SparseCore 0:
  32.8 82.5 all-reduce.1
  117.2 49.8 all-gather.4
  178.8 74.3 all-gather.6

commit v4 on v3

--- a/solution.py
+++ b/solution.py
@@ -273,14 +273,11 @@
     live_rows = jnp.arange(slab_rows, dtype=jnp.int32)[None, :] < child_count
     targets = jnp.where(live_rows, child_map, block_rows)
 
-    own_panel = front_panel.at[targets[0]].add(child_panel[0], mode="drop")
-    partner_top = jnp.zeros((panel_width, panel_cols), jnp.float32).at[targets[1]].add(
-        child_panel[1], mode="drop"
-    )
-    share = jnp.where(
-        row_id == 0,
-        own_panel[:panel_width],
-        jnp.where(row_id == 1 << top_bit, partner_top, 0.0),
+    is_root, is_partner = row_id == 0, row_id == 1 << top_bit
+    share = jnp.where(is_root, front_panel[:panel_width], 0.0)
+    share = share.at[jnp.where(is_partner, targets[1], targets[0])].add(
+        jnp.where(is_partner, child_panel[1], jnp.where(is_root, child_panel[0], 0.0)),
+        mode="drop",
     )
     diag_piece = lax.psum(share, "row")
 
@@ -288,13 +285,12 @@
     panel_slab = swapped(child_panel[1], "row", top_bit)
     half = slab_rows // 2
     early_slab = swapped(child_trail[1, :half], "row", top_bit)
-    late_slab = swapped(child_trail[1, half:], "row", top_bit)
-    panel = own_panel.at[partner_targets].add(panel_slab, mode="drop")
-    diag_piece, panel, early_slab = lax.optimization_barrier((diag_piece, panel, early_slab))
+    panel = front_panel.at[targets[0]].add(child_panel[0], mode="drop")
+    panel = panel.at[partner_targets].add(panel_slab, mode="drop")
+    diag_piece, panel, front_trail = lax.optimization_barrier((diag_piece, panel, front_trail))
     diag_full = lax.all_gather(diag_piece, "col", axis=0)
     trail = front_trail.at[targets[0]].add(child_trail[0], mode="drop")
     trail = trail.at[partner_targets[:half]].add(early_slab, mode="drop")
-    trail = trail.at[partner_targets[half:]].add(late_slab, mode="drop")
 
     window_rows = trail_cols * lax.axis_size("col")
     blank = jnp.zeros((window_rows, panel_cols), jnp.float32)
@@ -320,7 +316,12 @@
         window = window + arrived
         if level < top_bit:
             window, *state = lax.optimization_barrier((window, *state))
+        if level == top_bit - 1:
+            late_slab, _ = lax.optimization_barrier((child_trail[1, half:], arrived))
+            late_slab = swapped(late_slab, "row", top_bit)
     upper, inverse = state
+    late_slab, inverse, panel_full = lax.optimization_barrier((late_slab, inverse, panel_full))
+    trail = trail.at[partner_targets[half:]].add(late_slab, mode="drop")
     place = jnp.stack([(row_id == 0).astype(jnp.int32), col_id.astype(jnp.int32)])
     return update(place, panel_full, inverse, window, upper, trail)
 

time: 313 us -> 324 us (1.035)
  waiting for transfers between devices: 123 us -> 131 us
    ppermute x2, waiting for transfers between devices: 24.9 us -> 67.9 us  [on_device(): arrived = lax.ppermute(window, ('row', 'col'), route)]
    ppermute x4, waiting for transfers between devices: 80.7 us -> 47.5 us  [swapped(): return lax.ppermute(block, axis, route)]
    optimization_barrier x0 -> x1, local copies, waits for them, and re-layouts: none -> 6.17 us  [on_device(): lax.optimization_barrier((diag_piece, panel, front_trail))]
    unnamed x21, local copies, waits for them, and re-layouts: 14.3 us -> 8.22 us
  transfers between devices with their start and end apart: 10 -> 10, of which waited for: 4 -> 4; matrix products, arithmetic and copies ran while one was open for 19% -> 16% of each run, Pallas kernels for 20% -> 20%
where the time goes in v4:
time: 324 us; the launch traced here: 323 us
  waiting for transfers between devices  131 us (40%)
  Pallas kernels  89.4 us (28%)
  other arithmetic  56.6 us (17%)
  local copies, waits for them, and re-layouts  18.6 us (6%)
  between operations  13.9 us (4%)
  starting transfers between devices  13.7 us (4%)
    ppermute x2, waiting for transfers between devices, on_device(): arrived = lax.ppermute(window, ('row', 'col'), route)  67.9 us
    pallas_call x2, Pallas kernels, cholesky_part(): pl.pallas_call(kernel, out_shape=(shape, shape), in_specs=[pl.BlockSpec(m...  63.5 us
    ppermute x4, waiting for transfers between devices, swapped(): return lax.ppermute(block, axis, route)  47.5 us
    pallas_call x1, Pallas kernels, update(): pl.pallas_call(functools.partial(update_kernel, depth // size), grid_spec...  25.9 us
    psum x1, waiting for transfers between devices, on_device(): diag_piece = lax.psum(share, 'row')  15.5 us
    scatter-add x1, other arithmetic, on_device(): trail = front_trail.at[targets[0]].add(child_trail[0], mode='drop')  12.7 us
    scatter-add x1, other arithmetic, on_device(): trail = trail.at[partner_targets[half:]].add(late_slab, mode='drop')  8.91 us
    scatter-add x1, other arithmetic, on_device(): trail = trail.at[partner_targets[:half]].add(early_slab, mode='drop')  8.9 us
  transfers between devices with their start and end apart: 10, of which 4 were waited for; matrix products, arithmetic and copies ran while one was open for 16% of the time, Pallas kernels for 20%

profile of v4, /device:TPU:20, one launch (start us, length us, event | category | flops | bytes accessed | tf_op | source)
XLA Modules:
  0.0 323.1 jit_solution(11155877605126946042)
XLA Ops:
  7.2 0.0 all-reduce.2.cloned.1.call-start
  7.2 1.4 copy.17
  8.6 6.2 %copy.18 = f32[3072,512]{1,0:T(8,128)} copy(f32[3072,512]{1,0:T(8,128)} %param.7) | data formatting | bytes 12582912 | tf_op jit(solution)/shard_map/optimization_barrier | solution.py:290
  14.8 0.8 slice_bitcast_fusion.2
  15.6 0.3 collective-permute-start.1
  16.0 0.1 compare_select_fusion.2
  16.1 6.3 %scatter_custom_fusion = f32[1024,128]{1,0:T(8,128)S(1)} fusion(f32[1024,128]{1,0:T(8,128)S(1)} %slice_select_fusion, s32[1024]{0:T(1024)S(1)} %bitcast.42, f32[2,1024,128]{2,1,0:T(8,128)S(1)} %copy-done.5, f32[]{:T(128)} %constant.11.clone.1, pred[]{:T(512)S(6)} %eq.8, pred[]{:T(512)S(6)} %eq.7), kind=kCustom, calls=%fused_computation.20 | custom fusion | flops 393216 | bytes 1572870 | tf_op jit(solution)/shard_map/scatter-add | solution.py:278
  22.4 0.0 copy-start.6
  22.4 0.8 copy-done.6
  23.2 0.0 all-reduce.2.cloned.1.call-update
  23.2 0.0 all-gather.5.cloned.1.call-start
  23.3 2.7 collective-permute-start
  26.0 6.6 %scatter_custom_fusion.1 = f32[3072,128]{1,0:T(8,128)S(1)} fusion(f32[3072,128]{1,0:T(8,128)S(1)} %copy.17, s32[1024]{0:T(1024)S(1)} %bitcast.40, f32[2,1024,128]{2,1,0:T(8,128)S(1)} %copy-done.5), kind=kCustom, calls=%fused_computation.16 | custom fusion | flops 131072 | bytes 2097152 | tf_op jit(solution)/shard_map/scatter-add | solution.py:288
  32.6 14.7 %collective-permute-done = s32[1024]{0:T(1024)S(1)} collective-permute-done((s32[1024]{0:T(1024)S(1)}, s32[1024]{0:T(1024)S(1)}, u32[]{:S(2)}, u32[]{:S(2)}) %collective-permute-start) | collective-permute-done | bytes 4128 | tf_op jit(solution)/shard_map/ppermute | solution.py:250
  47.3 0.0 collective-permute-done.1
  47.3 7.0 %scatter_fusion = f32[3072,128]{1,0:T(8,128)S(1)} fusion(f32[3072,128]{1,0:T(8,128)S(1)} %scatter_custom_fusion.1, s32[1024]{0:T(1024)S(1)} %compare_select_fusion.3, f32[1024,128]{1,0:T(8,128)} %collective-permute-done.1), kind=kCustom, calls=%fused_computation.2 | custom fusion | flops 131072 | bytes 1576960 | tf_op jit(solution)/shard_map/scatter-add | solution.py:289
  54.3 0.0 copy-start.4
  54.3 15.5 %all-reduce.2.cloned.1.call-done = f32[1024,128]{1,0:T(8,128)} async-done(((f32[1024,128]{1,0:T(8,128)}), f32[1024,128]{1,0:T(8,128)}) %all-reduce.2.cloned.1.call-update) | async-done | bytes 524304 | tf_op jit(solution)/shard_map/psum | solution.py:282
  69.8 0.0 all-gather.5.cloned.1.call-update
  69.9 0.1 broadcast_in_dim.28
  70.0 3.6 %fusion.1 = f32[4096,128]{1,0:T(8,128)} fusion(s32[]{:T(128)S(6)} %max.3, f32[4096,128]{1,0:T(8,128)S(1)} %broadcast_in_dim.28, f32[3072,128]{1,0:T(8,128)S(1)} %scatter_fusion), kind=kLoop, calls=%fused_computation.10 | loop fusion | flops 1048576 | bytes 5767172 | tf_op jit(solution)/shard_map/concatenate | solution.py:298
  73.6 4.2 %all-to-all-start = ((f32[8,512,128]{2,1,0:T(8,128)}), f32[8,512,128]{2,1,0:T(8,128)S(1)}, u32[]{:S(2)}, u32[]{:S(2)}) async-start(f32[8,512,128]{2,1,0:T(8,128)} %bitcast.38), calls=%async_computation | async-start | bytes 4194304 | tf_op jit(solution)/shard_map/all_to_all | solution.py:303
  77.8 0.0 all-gather.7.cloned.1.call-start
  77.9 3.2 slice_bitcast_fusion
  81.0 0.9 collective-permute-start.2
  81.9 12.7 %scatter_custom_fusion.3 = f32[3072,512]{1,0:T(8,128)} fusion(f32[3072,512]{1,0:T(8,128)} %copy.18, s32[1024]{0:T(1024)S(1)} %bitcast.41, f32[2,1024,512]{2,1,0:T(8,128)} %param.9), kind=kCustom, calls=%fused_computation.11 | custom fusion | flops 524288 | bytes 8388608 | tf_op jit(solution)/shard_map/scatter-add | solution.py:292
  94.6 32.8 %collective-permute-done.2 = f32[512,512]{1,0:T(8,128)S(1)} collective-permute-done((f32[512,512]{1,0:T(8,128)}, f32[512,512]{1,0:T(8,128)S(1)}, u32[]{:S(2)}, u32[]{:S(2)}) %collective-permute-start.2) | collective-permute-done | bytes 1048608 | tf_op jit(solution)/shard_map/ppermute | solution.py:250
  127.4 8.9 %scatter_fusion.1 = f32[3072,512]{1,0:T(8,128)} fusion(f32[3072,512]{1,0:T(8,128)} %scatter_custom_fusion.3, s32[512]{0:T(512)S(1)} %get-tuple-element.55, f32[512,512]{1,0:T(8,128)S(1)} %collective-permute-done.2), kind=kCustom, calls=%fused_computation.4 | custom fusion | flops 262144 | bytes 3147776 | tf_op jit(solution)/shard_map/scatter-add | solution.py:293
  136.3 0.0 all-to-all-done
  136.3 0.0 all-gather.7.cloned.1.call-update
  136.4 0.6 pad_add_fusion.place_ref
  137.0 0.8 collective-permute-start.3
  137.8 2.2 copy-done.2
  140.0 35.8 %cholesky_and_inverse.2 = (f32[1024,1024]{1,0:T(8,128)S(1)}, f32[1024,1024]{1,0:T(8,128)S(1)}) custom-call(f32[8,1024,128]{2,1,0:T(8,128)S(1)} %bitcast.36), custom_call_target="tpu_custom_call" | custom-call | flops 30000001024 | bytes 12582912 | tf_op jit(solution)/shard_map/cholesky_and_inverse/pallas_call | solution.py:128
  175.7 0.0 copy-start.3
  175.7 0.0 collective-permute-done.3
  175.8 0.2 add.59
  176.0 1.8 copy-done.3
  177.7 0.0 copy-done.7
  177.8 3.3 %collective-permute-start.4 = (f32[512,512]{1,0:T(8,128)S(1)}, f32[512,512]{1,0:T(8,128)S(1)}, u32[]{:S(2)}, u32[]{:S(2)}) collective-permute-start(f32[512,512]{1,0:T(8,128)S(1)} %copy-done.7), channel_id=1, source_target_pairs={{0,16},{16,0},{8,24},{24,8},{1,17},{17,1},{9,25},{25,9},{2,18},{18... | collective-permute-start | bytes 3145736 | tf_op jit(solution)/shard_map/ppermute | solution.py:250
  181.1 1.5 collective-permute-start.5
  182.6 27.8 %cholesky_and_inverse.3 = (f32[1024,1024]{1,0:T(8,128)S(1)}, f32[1024,1024]{1,0:T(8,128)S(1)}) custom-call(f32[1024,1024]{1,0:T(8,128)S(1)} %get-tuple-element.38.upper_in, f32[1024,1024]{1,0:T(8,128)} %copy-done.3), custom_call_target="tpu_custom_call" | custom-call | flops 30000001024 | bytes 12582912 | tf_op jit(solution)/shard_map/cholesky_and_inverse/pallas_call | solution.py:128
  210.4 2.0 copy-done.1
  212.4 67.9 %collective-permute-done.5 = f32[8,512,128]{2,1,0:T(8,128)S(1)} collective-permute-done((f32[8,512,128]{2,1,0:T(8,128)S(1)}, f32[8,512,128]{2,1,0:T(8,128)S(1)}, u32[]{:S(2)}, u32[]{:S(2)}) %collective-permute-start.5) | collective-permute-done | bytes 2097184 | tf_op jit(solution)/shard_map/ppermute | solution.py:312
  280.2 1.5 add.60.window_ref
  281.8 0.0 collective-permute-done.4
  281.8 8.9 %scatter_fusion.2 = f32[3072,512]{1,0:T(8,128)} fusion(f32[3072,512]{1,0:T(8,128)} %scatter_fusion.1, s32[512]{0:T(512)S(1)} %get-tuple-element.54, f32[512,512]{1,0:T(8,128)S(1)} %collective-permute-done.4), kind=kCustom, calls=%fused_computation.5 | custom fusion | flops 262144 | bytes 3147776 | tf_op jit(solution)/shard_map/scatter-add | solution.py:324
  290.7 25.9 %factor_and_schur.1 = (f32[3072,128]{1,0:T(8,128)}, f32[3072,512]{1,0:T(8,128)}) custom-call(s32[2]{0:T(128)} %pad_add_fusion.place_ref, f32[8,3072,128]{2,1,0:T(8,128)} %bitcast.37, f32[1024,1024]{1,0:T(8,128)} %copy-done.1, f32[8,512,128]{2,1,0:T(8,128)} %add.60.window_ref, f32[1024,1024]{1,0:T(8,128)} %copy-done, f32[3072,512]{1,0:T(8,128)} %scatter_fusion.2), custom_call_target="tpu_custom_call" | custom-call | tf_op jit(solution)/shard_map/factor_and_schur/pallas_call | solution.py:215
  (19 shorter events, 0.1 us)
Async XLA Ops:
  7.2 62.7 %all-reduce.2.cloned.1.call-start = ((), (), s32[]{:S(2)}) async-start(), calls=%async_computation.1 | async-start | bytes 1048576 | tf_op jit(solution)/shard_map/psum | solution.py:282
  8.6 6.2 %copy-start.5 = (f32[2,1024,128]{2,1,0:T(8,128)S(1)}, f32[2,1024,128]{2,1,0:T(8,128)}, u32[]{:S(2)}) copy-start(f32[2,1024,128]{2,1,0:T(8,128)} %param.8) | copy-start | bytes 3145732
  14.8 1.2 copy-start.8
  14.8 1.2 copy-start.9
  15.6 31.7 %collective-permute-start.1 = (f32[1024,128]{1,0:T(8,128)}, f32[1024,128]{1,0:T(8,128)}, u32[]{:S(2)}, u32[]{:S(2)}) collective-permute-start(f32[1024,128]{1,0:T(8,128)} %slice_bitcast_fusion.2), channel_id=1, source_target_pairs={{0,16},{16,0},{8,24},{24,8},{1,17},{17,1},{9,25},{25,9},{2,18},{18... | collective-permute-start | bytes 1572872 | tf_op jit(solution)/shard_map/ppermute | solution.py:250
  22.4 0.8 copy-start.6
  23.2 113.1 %all-gather.5.cloned.1.call-start = ((), (), s32[]{:S(2)}) async-start(), calls=%async_computation.2 | async-start | bytes 4718592 | tf_op jit(solution)/shard_map/all_gather | solution.py:291
  23.3 24.0 %collective-permute-start = (s32[1024]{0:T(1024)S(1)}, s32[1024]{0:T(1024)S(1)}, u32[]{:S(2)}, u32[]{:S(2)}) collective-permute-start(s32[1024]{0:T(1024)S(1)} %bitcast.39), channel_id=1, source_target_pairs={{0,16},{16,0},{8,24},{24,8},{1,17},{17,1},{9,25},{25,9},{2,18},{18... | collective-permute-start | bytes 12296 | tf_op jit(solution)/shard_map/ppermute | solution.py:250
  54.3 19.3 %copy-start.4 = (f32[3072,128]{1,0:T(8,128)}, f32[3072,128]{1,0:T(8,128)S(1)}, u32[]{:S(2)}) copy-start(f32[3072,128]{1,0:T(8,128)S(1)} %scatter_fusion) | copy-start | bytes 4718596
  73.6 62.7 %all-to-all-start = ((f32[8,512,128]{2,1,0:T(8,128)}), f32[8,512,128]{2,1,0:T(8,128)S(1)}, u32[]{:S(2)}, u32[]{:S(2)}) async-start(f32[8,512,128]{2,1,0:T(8,128)} %bitcast.38), calls=%async_computation | async-start | bytes 4194304 | tf_op jit(solution)/shard_map/all_to_all | solution.py:303
  77.8 203.9 %all-gather.7.cloned.1.call-start = ((), (), s32[]{:S(2)}) async-start(), calls=%async_computation.3 | async-start | bytes 14155776 | tf_op jit(solution)/shard_map/all_gather | solution.py:306
  81.0 46.4 %collective-permute-start.2 = (f32[512,512]{1,0:T(8,128)}, f32[512,512]{1,0:T(8,128)S(1)}, u32[]{:S(2)}, u32[]{:S(2)}) collective-permute-start(f32[512,512]{1,0:T(8,128)} %get-tuple-element.50), channel_id=1, source_target_pairs={{0,16},{16,0},{8,24},{24,8},{1,17},{17,1},{9,25},{25,9},{2,18},{18... | collective-permute-start | bytes 3145736 | tf_op jit(solution)/shard_map/ppermute | solution.py:250
  137.0 38.8 %collective-permute-start.3 = (f32[8,512,128]{2,1,0:T(8,128)S(1)}, f32[8,512,128]{2,1,0:T(8,128)S(1)}, u32[]{:S(2)}, u32[]{:S(2)}) collective-permute-start(f32[8,512,128]{2,1,0:T(8,128)S(1)} %all-to-all-done), channel_id=1, source_target_pairs={{0,16},{1,17},{2,18},{3,19},{12,28},{13,29},{14,30},{15,31}} | collective-permute-start | bytes 6291464 | tf_op jit(solution)/shard_map/ppermute | solution.py:312
  137.8 2.2 copy-start.2
  175.7 2.0 copy-start.3
  175.7 2.0 copy-start.7
  177.8 104.0 %collective-permute-start.4 = (f32[512,512]{1,0:T(8,128)S(1)}, f32[512,512]{1,0:T(8,128)S(1)}, u32[]{:S(2)}, u32[]{:S(2)}) collective-permute-start(f32[512,512]{1,0:T(8,128)S(1)} %copy-done.7), channel_id=1, source_target_pairs={{0,16},{16,0},{8,24},{24,8},{1,17},{17,1},{9,25},{25,9},{2,18},{18... | collective-permute-start | bytes 3145736 | tf_op jit(solution)/shard_map/ppermute | solution.py:250
  181.1 99.2 %collective-permute-start.5 = (f32[8,512,128]{2,1,0:T(8,128)S(1)}, f32[8,512,128]{2,1,0:T(8,128)S(1)}, u32[]{:S(2)}, u32[]{:S(2)}) collective-permute-start(f32[8,512,128]{2,1,0:T(8,128)S(1)} %add.59), channel_id=1, source_target_pairs={{0,8},{16,24},{1,9},{17,25},{2,10},{18,26},{3,11},{19,27},{12,4},{... | collective-permute-start | bytes 6291464 | tf_op jit(solution)/shard_map/ppermute | solution.py:312
  210.3 2.0 copy-start.1
  212.4 69.4 %copy-start = (f32[1024,1024]{1,0:T(8,128)}, f32[1024,1024]{1,0:T(8,128)S(1)}, u32[]{:S(2)}) copy-start(f32[1024,1024]{1,0:T(8,128)S(1)} %get-tuple-element.47.upper_ref) | copy-start | bytes 12582916
Sparse Core Ops, SparseCore 0:
  23.4 46.4 all-reduce.1
  71.7 49.8 all-gather.4
  136.5 74.5 all-gather.6

commit v5 on v4

--- a/solution.py
+++ b/solution.py
@@ -236,6 +236,11 @@
             jax.ShapeDtypeStruct((rows, width), jnp.float32),
         ),
         compiler_params=pltpu.CompilerParams(vmem_limit_bytes=56 << 20),
+        cost_estimate=pl.CostEstimate(
+            flops=6 * rows * depth * (width + narrow) + 12 * depth * depth * width,
+            bytes_accessed=4 * rows * (depth + 2 * (width + narrow)),
+            transcendentals=0,
+        ),
         name="factor_and_schur",
     )(place, panel, inverse, window, upper, trail)
 
@@ -316,14 +321,16 @@
         window = window + arrived
         if level < top_bit:
             window, *state = lax.optimization_barrier((window, *state))
-        if level == top_bit - 1:
-            late_slab, _ = lax.optimization_barrier((child_trail[1, half:], arrived))
-            late_slab = swapped(late_slab, "row", top_bit)
+    panel_full, window = lax.optimization_barrier((panel_full, window))
     upper, inverse = state
-    late_slab, inverse, panel_full = lax.optimization_barrier((late_slab, inverse, panel_full))
-    trail = trail.at[partner_targets[half:]].add(late_slab, mode="drop")
+
+    late_slab, window = lax.optimization_barrier((child_trail[1, half:], window))
+    late_slab = swapped(late_slab, "row", top_bit)
     place = jnp.stack([(row_id == 0).astype(jnp.int32), col_id.astype(jnp.int32)])
-    return update(place, panel_full, inverse, window, upper, trail)
+    factor_block, schur_block = update(place, panel_full, inverse, window, upper, trail)
+    late_slab, schur_block = lax.optimization_barrier((late_slab, schur_block))
+    schur_block = schur_block.at[partner_targets[half:]].add(late_slab, mode="drop")
+    return factor_block, schur_block
 
 
 def solution(mesh):

time: 324 us -> 299 us (0.923)
  waiting for transfers between devices: 131 us -> 104 us
  starting transfers between devices: 13.7 us -> 10.4 us
    ppermute x2, waiting for transfers between devices: 67.9 us -> 24.7 us  [on_device(): arrived = lax.ppermute(window, ('row', 'col'), route)]
    ppermute x4, waiting for transfers between devices: 47.5 us -> 63.8 us  [swapped(): return lax.ppermute(block, axis, route)]
    ppermute x4, starting transfers between devices: 7.14 us -> 3.85 us  [swapped(): return lax.ppermute(block, axis, route)]
  transfers between devices with their start and end apart: 10 -> 10, of which waited for: 4 -> 5; matrix products, arithmetic and copies ran while one was open for 16% -> 17% of each run, Pallas kernels for 20% -> 30%
where the time goes in v5:
time: 299 us; the launch traced here: 295 us
  waiting for transfers between devices  104 us (35%)
  Pallas kernels  89.4 us (30%)
  other arithmetic  56.9 us (19%)
  local copies, waits for them, and re-layouts  20.6 us (7%)
  between operations  13.9 us (5%)
  starting transfers between devices  10.4 us (3%)
    ppermute x4, waiting for transfers between devices, swapped(): return lax.ppermute(block, axis, route)  63.8 us
    pallas_call x2, Pallas kernels, cholesky_part(): pl.pallas_call(kernel, out_shape=(shape, shape), in_specs=[pl.BlockSpec(m...  63.5 us
    pallas_call x1, Pallas kernels, update(): pl.pallas_call(functools.partial(update_kernel, depth // size), grid_spec...  25.9 us
    ppermute x2, waiting for transfers between devices, on_device(): arrived = lax.ppermute(window, ('row', 'col'), route)  24.7 us
    psum x1, waiting for transfers between devices, on_device(): diag_piece = lax.psum(share, 'row')  15.5 us
    scatter-add x1, other arithmetic, on_device(): trail = front_trail.at[targets[0]].add(child_trail[0], mode='drop')  12.7 us
    unnamed x21, local copies, waits for them, and re-layouts  10.2 us
    scatter-add x1, other arithmetic, on_device(): schur_block.at[partner_targets[half:]].add(late_slab, mode='drop')  9.29 us
  transfers between devices with their start and end apart: 10, of which 5 were waited for; matrix products, arithmetic and copies ran while one was open for 17% of the time, Pallas kernels for 30%

profile of v5, /device:TPU:20, one launch (start us, length us, event | category | flops | bytes accessed | tf_op | source)
XLA Modules:
  0.0 295.3 jit_solution(1580224309427877219)
XLA Ops:
  7.2 0.0 all-reduce.2.cloned.1.call-start
  7.2 1.4 copy.17
  8.6 6.2 %copy.18 = f32[3072,512]{1,0:T(8,128)} copy(f32[3072,512]{1,0:T(8,128)} %param.7) | data formatting | bytes 12582912 | tf_op jit(solution)/shard_map/optimization_barrier | solution.py:295
  14.8 0.8 slice_bitcast_fusion.2
  15.6 0.3 collective-permute-start.1
  16.0 0.1 compare_select_fusion.2
  16.1 6.3 %scatter_custom_fusion = f32[1024,128]{1,0:T(8,128)S(1)} fusion(f32[1024,128]{1,0:T(8,128)S(1)} %slice_select_fusion, s32[1024]{0:T(1024)S(1)} %bitcast.41, f32[2,1024,128]{2,1,0:T(8,128)S(1)} %copy-done.5, f32[]{:T(128)} %constant.11.clone.1, pred[]{:T(512)S(6)} %eq.8, pred[]{:T(512)S(6)} %eq.7), kind=kCustom, calls=%fused_computation.20 | custom fusion | flops 393216 | bytes 1572870 | tf_op jit(solution)/shard_map/scatter-add | solution.py:283
  22.4 0.0 copy-start.6
  22.4 0.8 copy-done.6
  23.2 0.0 all-reduce.2.cloned.1.call-update
  23.2 0.0 all-gather.5.cloned.1.call-start
  23.3 2.7 collective-permute-start
  26.0 6.6 %scatter_custom_fusion.1 = f32[3072,128]{1,0:T(8,128)S(1)} fusion(f32[3072,128]{1,0:T(8,128)S(1)} %copy.17, s32[1024]{0:T(1024)S(1)} %bitcast.39, f32[2,1024,128]{2,1,0:T(8,128)S(1)} %copy-done.5), kind=kCustom, calls=%fused_computation.16 | custom fusion | flops 131072 | bytes 2097152 | tf_op jit(solution)/shard_map/scatter-add | solution.py:293
  32.6 14.7 %collective-permute-done = s32[1024]{0:T(1024)S(1)} collective-permute-done((s32[1024]{0:T(1024)S(1)}, s32[1024]{0:T(1024)S(1)}, u32[]{:S(2)}, u32[]{:S(2)}) %collective-permute-start) | collective-permute-done | bytes 4128 | tf_op jit(solution)/shard_map/ppermute | solution.py:255
  47.3 0.0 collective-permute-done.1
  47.3 7.0 %scatter_fusion = f32[3072,128]{1,0:T(8,128)S(1)} fusion(f32[3072,128]{1,0:T(8,128)S(1)} %scatter_custom_fusion.1, s32[1024]{0:T(1024)S(1)} %compare_select_fusion.3, f32[1024,128]{1,0:T(8,128)} %collective-permute-done.1), kind=kCustom, calls=%fused_computation.2 | custom fusion | flops 131072 | bytes 1576960 | tf_op jit(solution)/shard_map/scatter-add | solution.py:294
  54.3 0.0 copy-start.4
  54.3 15.5 %all-reduce.2.cloned.1.call-done = f32[1024,128]{1,0:T(8,128)} async-done(((f32[1024,128]{1,0:T(8,128)}), f32[1024,128]{1,0:T(8,128)}) %all-reduce.2.cloned.1.call-update) | async-done | bytes 524304 | tf_op jit(solution)/shard_map/psum | solution.py:287
  69.8 0.0 all-gather.5.cloned.1.call-update
  69.9 0.1 broadcast_in_dim.28
  70.0 3.6 %fusion.1 = f32[4096,128]{1,0:T(8,128)} fusion(s32[]{:T(128)S(6)} %max.3, f32[4096,128]{1,0:T(8,128)S(1)} %broadcast_in_dim.28, f32[3072,128]{1,0:T(8,128)S(1)} %scatter_fusion), kind=kLoop, calls=%fused_computation.10 | loop fusion | flops 1048576 | bytes 5767172 | tf_op jit(solution)/shard_map/concatenate | solution.py:303
  73.6 4.2 %all-to-all-start = ((f32[8,512,128]{2,1,0:T(8,128)}), f32[8,512,128]{2,1,0:T(8,128)S(1)}, u32[]{:S(2)}, u32[]{:S(2)}) async-start(f32[8,512,128]{2,1,0:T(8,128)} %bitcast.37), calls=%async_computation | async-start | bytes 4194304 | tf_op jit(solution)/shard_map/all_to_all | solution.py:308
  77.8 0.0 all-gather.7.cloned.1.call-start
  77.8 3.2 %slice_bitcast_fusion = (f32[512,512]{1,0:T(8,128)}, f32[512,512]{1,0:T(8,128)}) fusion(f32[2,1024,512]{2,1,0:T(8,128)} %param.9), kind=kLoop, calls=%fused_computation.14 | loop fusion | bytes 4194304 | tf_op jit(solution)/shard_map/squeeze | solution.py:327
  81.1 0.9 collective-permute-start.2
  81.9 12.7 %scatter_custom_fusion.3 = f32[3072,512]{1,0:T(8,128)} fusion(f32[3072,512]{1,0:T(8,128)} %copy.18, s32[1024]{0:T(1024)S(1)} %bitcast.40, f32[2,1024,512]{2,1,0:T(8,128)} %param.9), kind=kCustom, calls=%fused_computation.11 | custom fusion | flops 524288 | bytes 8388608 | tf_op jit(solution)/shard_map/scatter-add | solution.py:297
  94.6 32.8 %collective-permute-done.2 = f32[512,512]{1,0:T(8,128)S(1)} collective-permute-done((f32[512,512]{1,0:T(8,128)}, f32[512,512]{1,0:T(8,128)S(1)}, u32[]{:S(2)}, u32[]{:S(2)}) %collective-permute-start.2) | collective-permute-done | bytes 1048608 | tf_op jit(solution)/shard_map/ppermute | solution.py:255
  127.4 8.9 %scatter_fusion.1 = f32[3072,512]{1,0:T(8,128)} fusion(f32[3072,512]{1,0:T(8,128)} %scatter_custom_fusion.3, s32[512]{0:T(512)S(1)} %get-tuple-element.63, f32[512,512]{1,0:T(8,128)S(1)} %collective-permute-done.2), kind=kCustom, calls=%fused_computation.4 | custom fusion | flops 262144 | bytes 3147776 | tf_op jit(solution)/shard_map/scatter-add | solution.py:298
  136.3 0.0 all-to-all-done
  136.3 0.0 all-gather.7.cloned.1.call-update
  136.4 0.6 pad_add_fusion.place_ref
  137.0 0.8 collective-permute-start.3
  137.8 2.2 copy-done
  139.9 35.7 %cholesky_and_inverse.2 = (f32[1024,1024]{1,0:T(8,128)S(1)}, f32[1024,1024]{1,0:T(8,128)S(1)}) custom-call(f32[8,1024,128]{2,1,0:T(8,128)S(1)} %bitcast.36), custom_call_target="tpu_custom_call" | custom-call | flops 30000001024 | bytes 12582912 | tf_op jit(solution)/shard_map/cholesky_and_inverse/pallas_call | solution.py:128
  175.7 0.0 copy-start.3
  175.7 0.0 collective-permute-done.3
  175.7 0.2 add.59
  175.9 1.8 copy-done.3
  177.7 1.5 collective-permute-start.4
  179.2 27.8 %cholesky_and_inverse.3 = (f32[1024,1024]{1,0:T(8,128)S(1)}, f32[1024,1024]{1,0:T(8,128)S(1)}) custom-call(f32[1024,1024]{1,0:T(8,128)S(1)} %get-tuple-element.42.upper_in, f32[1024,1024]{1,0:T(8,128)} %copy-done.3), custom_call_target="tpu_custom_call" | custom-call | flops 30000001024 | bytes 12582912 | tf_op jit(solution)/shard_map/cholesky_and_inverse/pallas_call | solution.py:128
  207.0 2.0 copy-done.1
  209.0 2.0 copy-done.2
  211.0 24.7 %collective-permute-done.4 = f32[8,512,128]{2,1,0:T(8,128)S(1)} collective-permute-done((f32[8,512,128]{2,1,0:T(8,128)S(1)}, f32[8,512,128]{2,1,0:T(8,128)S(1)}, u32[]{:S(2)}, u32[]{:S(2)}) %collective-permute-start.4) | collective-permute-done | bytes 2097184 | tf_op jit(solution)/shard_map/ppermute | solution.py:317
  235.8 1.5 add.60.window_ref
  237.3 0.0 collective-permute-start.5
  237.3 25.9 %factor_and_schur.1 = (f32[3072,128]{1,0:T(8,128)}, f32[3072,512]{1,0:T(8,128)}) custom-call(s32[2]{0:T(128)} %pad_add_fusion.place_ref, f32[8,3072,128]{2,1,0:T(8,128)} %bitcast.43, f32[1024,1024]{1,0:T(8,128)} %copy-done.2, f32[8,512,128]{2,1,0:T(8,128)} %add.60.window_ref, f32[1024,1024]{1,0:T(8,128)} %copy-done.1, f32[3072,512]{1,0:T(8,128)} %scatter_fusion.1), custom_call_target="tpu_custom_call" | custom-call | flops 18522046464 | bytes 28311552 | tf_op jit(solution)/shard_map/factor_and_schur/pallas_call | solution.py:215
  263.2 16.3 %collective-permute-done.5 = f32[512,512]{1,0:T(8,128)S(1)} collective-permute-done((f32[512,512]{1,0:T(8,128)S(1)}, f32[512,512]{1,0:T(8,128)S(1)}, u32[]{:S(2)}, u32[]{:S(2)}) %collective-permute-start.5) | collective-permute-done | bytes 1048608 | tf_op jit(solution)/shard_map/ppermute | solution.py:255
  279.5 9.3 %scatter_fusion.2 = f32[3072,512]{1,0:T(8,128)} fusion(f32[3072,512]{1,0:T(8,128)} %get-tuple-element.56, s32[512]{0:T(512)S(1)} %get-tuple-element.62, f32[512,512]{1,0:T(8,128)S(1)} %collective-permute-done.5), kind=kCustom, calls=%fused_computation.5 | custom fusion | flops 262144 | bytes 3147776 | tf_op jit(solution)/shard_map/scatter-add | solution.py:332
  (19 shorter events, 0.1 us)
Async XLA Ops:
  7.2 62.7 %all-reduce.2.cloned.1.call-start = ((), (), s32[]{:S(2)}) async-start(), calls=%async_computation.1 | async-start | bytes 1048576 | tf_op jit(solution)/shard_map/psum | solution.py:287
  8.6 6.2 %copy-start.5 = (f32[2,1024,128]{2,1,0:T(8,128)S(1)}, f32[2,1024,128]{2,1,0:T(8,128)}, u32[]{:S(2)}) copy-start(f32[2,1024,128]{2,1,0:T(8,128)} %param.8) | copy-start | bytes 3145732
  14.8 1.2 copy-start.8
  14.8 1.2 copy-start.9
  15.6 31.7 %collective-permute-start.1 = (f32[1024,128]{1,0:T(8,128)}, f32[1024,128]{1,0:T(8,128)}, u32[]{:S(2)}, u32[]{:S(2)}) collective-permute-start(f32[1024,128]{1,0:T(8,128)} %slice_bitcast_fusion.2), channel_id=1, source_target_pairs={{0,16},{16,0},{8,24},{24,8},{1,17},{17,1},{9,25},{25,9},{2,18},{18... | collective-permute-start | bytes 1572872 | tf_op jit(solution)/shard_map/ppermute | solution.py:255
  22.4 0.8 copy-start.6
  23.2 113.1 %all-gather.5.cloned.1.call-start = ((), (), s32[]{:S(2)}) async-start(), calls=%async_computation.2 | async-start | bytes 4718592 | tf_op jit(solution)/shard_map/all_gather | solution.py:296
  23.3 24.0 %collective-permute-start = (s32[1024]{0:T(1024)S(1)}, s32[1024]{0:T(1024)S(1)}, u32[]{:S(2)}, u32[]{:S(2)}) collective-permute-start(s32[1024]{0:T(1024)S(1)} %bitcast.38), channel_id=1, source_target_pairs={{0,16},{16,0},{8,24},{24,8},{1,17},{17,1},{9,25},{25,9},{2,18},{18... | collective-permute-start | bytes 12296 | tf_op jit(solution)/shard_map/ppermute | solution.py:255
  54.3 19.3 %copy-start.4 = (f32[3072,128]{1,0:T(8,128)}, f32[3072,128]{1,0:T(8,128)S(1)}, u32[]{:S(2)}) copy-start(f32[3072,128]{1,0:T(8,128)S(1)} %scatter_fusion) | copy-start | bytes 4718596
  73.6 62.7 %all-to-all-start = ((f32[8,512,128]{2,1,0:T(8,128)}), f32[8,512,128]{2,1,0:T(8,128)S(1)}, u32[]{:S(2)}, u32[]{:S(2)}) async-start(f32[8,512,128]{2,1,0:T(8,128)} %bitcast.37), calls=%async_computation | async-start | bytes 4194304 | tf_op jit(solution)/shard_map/all_to_all | solution.py:308
  77.8 159.4 %all-gather.7.cloned.1.call-start = ((), (), s32[]{:S(2)}) async-start(), calls=%async_computation.3 | async-start | bytes 14155776 | tf_op jit(solution)/shard_map/all_gather | solution.py:311
  81.1 46.4 %collective-permute-start.2 = (f32[512,512]{1,0:T(8,128)}, f32[512,512]{1,0:T(8,128)S(1)}, u32[]{:S(2)}, u32[]{:S(2)}) collective-permute-start(f32[512,512]{1,0:T(8,128)} %get-tuple-element.59), channel_id=1, source_target_pairs={{0,16},{16,0},{8,24},{24,8},{1,17},{17,1},{9,25},{25,9},{2,18},{18... | collective-permute-start | bytes 3145736 | tf_op jit(solution)/shard_map/ppermute | solution.py:255
  137.0 38.8 %collective-permute-start.3 = (f32[8,512,128]{2,1,0:T(8,128)S(1)}, f32[8,512,128]{2,1,0:T(8,128)S(1)}, u32[]{:S(2)}, u32[]{:S(2)}) collective-permute-start(f32[8,512,128]{2,1,0:T(8,128)S(1)} %all-to-all-done), channel_id=1, source_target_pairs={{0,16},{1,17},{2,18},{3,19},{12,28},{13,29},{14,30},{15,31}} | collective-permute-start | bytes 6291464 | tf_op jit(solution)/shard_map/ppermute | solution.py:317
  137.8 2.2 copy-start
  175.7 2.0 copy-start.3
  177.7 58.0 %collective-permute-start.4 = (f32[8,512,128]{2,1,0:T(8,128)S(1)}, f32[8,512,128]{2,1,0:T(8,128)S(1)}, u32[]{:S(2)}, u32[]{:S(2)}) collective-permute-start(f32[8,512,128]{2,1,0:T(8,128)S(1)} %add.59), channel_id=1, source_target_pairs={{0,8},{16,24},{1,9},{17,25},{2,10},{18,26},{3,11},{19,27},{12,4},{... | collective-permute-start | bytes 6291464 | tf_op jit(solution)/shard_map/ppermute | solution.py:317
  207.0 2.0 copy-start.1
  209.0 2.0 copy-start.2
  235.8 1.5 copy-start.7
  237.3 42.2 %collective-permute-start.5 = (f32[512,512]{1,0:T(8,128)S(1)}, f32[512,512]{1,0:T(8,128)S(1)}, u32[]{:S(2)}, u32[]{:S(2)}) collective-permute-start(f32[512,512]{1,0:T(8,128)S(1)} %copy-done.7), channel_id=1, source_target_pairs={{0,16},{16,0},{8,24},{24,8},{1,17},{17,1},{9,25},{25,9},{2,18},{18... | collective-permute-start | bytes 3145736 | tf_op jit(solution)/shard_map/ppermute | solution.py:255
Sparse Core Ops, SparseCore 0:
  23.4 46.4 all-reduce.1
  71.7 49.8 all-gather.4
  136.5 74.5 all-gather.6
